TPU v7x, 128 devices: a whole 4x4x4 slice. The times are simulated.
128 devices in a mesh: obs: 8 (over x, z_lo), par: 16 (over z_hi, y, core).
Axes of the slice: x: 4, y: 4, z: 4 (z_hi: 2, z_lo: 2; z = z_hi * 2 + z_lo), core: 2. Of those that a mesh axis runs over, the one named last changes fastest.
Arguments:
- jacobian: float32 [3584, 10240], P('obs', 'par'), may hold values from -0.09375 to 0.09375
- obs_group: int32 [3584], P('obs'), may hold values from 0 to 2
- group_weight: float32 [3], replicated, may hold values from 0.5 to 4
- misfit: float32 [3584], P('obs'), may hold values from -6 to 6
Outputs:
- normal_matrix: float32 [10240, 10240], P('obs', 'par')
- gradient: float32 [10240], P('par')
All inputs are finite; a program needn't handle non-finite values.
Results may differ from a plain program's by a relative error of at most 0.00013.
Values sent between devices are 32-bit elements; how exact they have to be, the bound alone decides.
No kernel may reach another device: no remote copies, remote signals or barrier semaphores. Data moves between devices by JAX's collectives and lax.ppermute only.
A program may use at most 128 MiB of HBM per device.

v0:
```python
import jax
import jax.numpy as jnp
from jax import lax
from jax.sharding import PartitionSpec as P


def contract_rows(left, right):
    return lax.dot_general(
        left,
        right,
        (((0,), (0,)), ((), ())),
        precision=lax.Precision.HIGHEST,
        preferred_element_type=jnp.float32,
    )


def body(jacobian, obs_group, group_weight, misfit):
    levels = jnp.arange(group_weight.shape[0], dtype=jnp.int32)
    onehot = (obs_group[:, None] == levels[None, :]).astype(jnp.float32)
    weight_row = jnp.sum(onehot * group_weight[None, :], axis=1)
    weighted = jacobian * weight_row[:, None]
    gathered = lax.all_gather(jacobian, "par", axis=1, tiled=True)
    partial_term = contract_rows(gathered, weighted)
    normal_matrix = lax.psum_scatter(partial_term, "obs", scatter_dimension=0, tiled=True)
    local_grad = jnp.dot(
        weight_row * misfit,
        jacobian,
        precision=lax.Precision.HIGHEST,
        preferred_element_type=jnp.float32,
    )
    gradient = lax.psum(local_grad, "obs")
    return (normal_matrix, gradient)


def solution(mesh):
    return jax.shard_map(
        body,
        mesh=mesh,
        in_specs=(P("obs", "par"), P("obs"), P(), P("obs")),
        out_specs=(P("obs", "par"), P("par")),
        check_vma=False,
    )
```

profile of v0, /device:TPU:39, one launch (start us, length us, event | category | flops | bytes accessed | tf_op | source)
XLA Modules:
  0.0 688.9 jit_solution(13422391461350485784)
XLA Ops:
  7.2 0.0 copy-start
  7.2 0.0 copy-start.2
  7.2 0.0 copy-start.3
  7.2 0.0 all-gather.2.cloned.1.call-start
  7.2 0.7 all-gather.2.cloned.1.call-update
  7.9 0.0 reduce-scatter.2.cloned.1.call-start
  8.0 0.0 copy-done.2
  8.0 0.0 copy-done.3
  8.0 0.1 select_reduce_fusion
  8.1 120.8 %all-gather.2.cloned.1.call-done = f32[448,10240]{1,0:T(8,128)} async-done(((f32[448,640]{1,0:T(8,128)}), f32[448,10240]{1,0:T(8,128)}) %all-gather.2.cloned.1.call-update) | async-done | bytes 18350096 | tf_op jit(solution)/shard_map/all_gather | solution.py:22
  128.9 0.0 copy-done
  128.9 47.2 %convolution_bitcast_fusion = f32[10240,640]{0,1:T(8,128)} fusion(f32[448,10240]{1,0:T(8,128)} %all-gather.2.cloned.1.call-done, f32[448,640]{1,0:T(8,128)S(1)} %copy-done, f32[448]{0:T(512)S(1)} %select_reduce_fusion), kind=kOutput, calls=%fused_computation | convolution fusion | flops 35232440320 | bytes 45713152 | tf_op jit(solution)/shard_map/dot_general | solution.py:8
  176.1 0.0 copy-start.1
  176.1 0.0 reduce-scatter.2.cloned.1.call-update
  176.1 0.7 copy-done.1
  176.8 0.7 convolution_reduce_fusion
  177.5 29.3 %psum.7 = f32[640]{0:T(1024)} all-reduce(f32[640]{0:T(1024)S(1)} %convolution_reduce_fusion), channel_id=1, replica_groups=mesh['obs'=8,'par'=16] {'obs'}, use_global_device_ids=true, to_apply=%region_2.0 | all-reduce | flops 640 | bytes 5120 | tf_op jit(solution)/shard_map/psum | solution.py:31
  206.8 470.7 %reduce-scatter.2.cloned.1.call-done = f32[1280,640]{0,1:T(8,128)} async-done(((f32[10240,640]{0,1:T(8,128)}), f32[1280,640]{0,1:T(8,128)}) %reduce-scatter.2.cloned.1.call-update) | async-done | bytes 3276816 | tf_op jit(solution)/shard_map/reduce_scatter | solution.py:24
  677.5 4.6 copy.7
  (1 shorter events, 0.0 us)
Async XLA Ops:
  7.2 121.7 %copy-start = (f32[448,640]{1,0:T(8,128)S(1)}, f32[448,640]{1,0:T(8,128)}, u32[]{:S(2)}) copy-start(f32[448,640]{1,0:T(8,128)} %param.4) | copy-start | bytes 3440644
  7.2 0.8 copy-start.2
  7.2 0.8 copy-start.3
  7.2 121.7 %all-gather.2.cloned.1.call-start = ((), (), s32[]{:S(2)}) async-start(), calls=%async_computation.1 | async-start | bytes 19496960 | tf_op jit(solution)/shard_map/all_gather | solution.py:22
  7.9 669.6 %reduce-scatter.2.cloned.1.call-start = ((), (), s32[]{:S(2)}) async-start(), calls=%async_computation.2 | async-start | bytes 29491200 | tf_op jit(solution)/shard_map/reduce_scatter | solution.py:24
  176.1 0.7 copy-start.1
Sparse Core Ops, SparseCore 0:
  10.5 118.3 all-gather.1
  176.2 501.2 reduce-scatter.1
where the time goes:
time: 692 us; the launch traced here: 689 us
  waiting for transfers between devices  592 us (86%)
  matrix products  47.9 us (7%)
  blocking collectives  29.3 us (4%)
  between operations  14.1 us (2%)
    reduce_scatter x1, waiting for transfers between devices, body(): lax.psum_scatter(partial_term, 'obs', scatter_dimension=0, tiled=True)  471 us
    all_gather x1, waiting for transfers between devices, body(): gathered = lax.all_gather(jacobian, 'par', axis=1, tiled=True)  121 us
    dot_general x1, matrix products, contract_rows(): lax.dot_general(left, right, (((0,), (0,)), ((), ())), precision=lax.Prec...  47.2 us
    psum x1, blocking collectives, body(): gradient = lax.psum(local_grad, 'obs')  29.3 us
  transfers between devices with their start and end apart: 2, of which 2 were waited for; matrix products, arithmetic and copies ran while one was open for 0% of the time, Pallas kernels for 0%

commit v1 on v0

v1 whole, which is shorter than its diff:
```python
import functools

import jax
import jax.numpy as jnp
from jax import lax
from jax.experimental import pallas as pl
from jax.experimental.pallas import tpu as pltpu
from jax.sharding import Mesh, PartitionSpec as P

NAMES = ("x", "zlo", "zhi", "y", "core")
SIZES = (4, 2, 2, 4, 2)
X, ZLO, ZHI, Y, CORE = SIZES
PHASES = (96, 128)
TILE = 8
ORDER = (
    ('X1',),
    ('T1a',),
    ('T2a', 'T1a'),
    ('T1b', 'T1a'),
    ('Z', 'X1'),
    ('NOa', 'T2a'),
    ('ZHa', 'T2a'),
    ('T2b', 'T1b'),
    ('X2', 'X1'),
    ('FOa', 'NOa'),
    ('NPa', 'ZHa'),
    ('ZHb', 'T2b'),
    ('NOb', 'T2b'),
    ('V1', 'Z'),
    ('FPa', 'NPa', 'FOa'),
    ('FOb', 'NOb', 'FPa', 'X2'),
    ('NPb', 'ZHb', 'V1'),
    ('V2', 'V1'),
    ('FPb', 'NPb', 'FOb'),
)


def linear(x, zlo, zhi, y, core):
    return (((x * ZLO + zlo) * ZHI + zhi) * Y + y) * CORE + core


def send(value, target):
    pairs = []
    for x in range(X):
        for zlo in range(ZLO):
            for zhi in range(ZHI):
                for y in range(Y):
                    for core in range(CORE):
                        there = target(x, zlo, zhi, y, core)
                        pairs.append((linear(x, zlo, zhi, y, core), linear(*there)))
    return lax.ppermute(value, NAMES, pairs)


NEAR, FAR = (1, 3), (3, 1)


def flip_x(masks):
    return lambda x, zlo, zhi, y, core: (x ^ masks[core], zlo, zhi, y, core)


def flip_y(masks):
    return lambda x, zlo, zhi, y, core: (x, zlo, zhi, y ^ masks[core], core)


def flip_zlo(x, zlo, zhi, y, core):
    return x, zlo ^ 1, zhi, y, core


def flip_zhi(x, zlo, zhi, y, core):
    return x, zlo, zhi ^ 1, y, core


def flip_core(x, zlo, zhi, y, core):
    return x, zlo, zhi, y, core ^ 1


def spread_yz(x, zlo, zhi, y, core):
    y = y ^ (2 * ((x & 1) ^ core) + zlo)
    return x, zlo ^ (y & 1), zhi ^ (x >> 1) ^ core, y, core


def spread_x(x, zlo, zhi, y, core):
    return x ^ (2 * (zhi ^ core) + ((y >> 1) ^ core)), zlo, zhi, y, core


def in_two(value):
    high = value.astype(jnp.bfloat16)
    return high, (value - high.astype(jnp.float32)).astype(jnp.bfloat16)


def dot(a, b):
    return lax.dot_general(a, b, (((0,), (0,)), ((), ())), preferred_element_type=jnp.float32)


def contract(left, right):
    left_high, left_low = in_two(left.reshape(-1, left.shape[-1]))
    right_high, right_low = in_two(right.reshape(-1, right.shape[-1]))
    return dot(left_high, right_high) + (dot(left_low, right_high) + dot(left_high, right_low))


def accumulate(low, steps, pick_ref, *refs):
    lefts, rights = refs[: len(low)], refs[len(low) : len(low) + ZLO]
    out_ref, rest = refs[-1], refs[len(low) + ZLO : -1]
    step = pl.program_id(1)

    @pl.when(step == 0)
    def _():
        out_ref[...] = rest[0][...] if rest else jnp.zeros_like(out_ref)

    for which in range(ZLO):
        if steps[which]:

            @pl.when(step // 2 == which if all(steps) else step >= 0)
            def _():
                out_ref[0] += functools.reduce(
                    lambda p, q: p + q,
                    [
                        contract(lefts[k][0], rights[which][:, low[k] : low[k] + lefts[k].shape[2]])
                        for k in steps[which]
                    ],
                )


def product(lefts, low, panels, sides, total, steps):
    wide = panels[0].shape[-1]
    columns = wide // CORE
    count = panels[0].shape[1] // TILE * TILE
    n = sides.shape[0]
    block = pl.BlockSpec((1, wide, columns), lambda s, i, pick: (pick[s], 0, 0))
    rows = sum(left.shape[2] for left in lefts)
    both = all(steps)
    alone = 0 if steps[0] else 1

    def left_spec(k, left):
        always = [which for which in range(ZLO) if k in steps[which]]
        if len(always) == 2:
            index = lambda s, i, pick: (i // 2, i % 2, 0, 0)
        else:
            index = lambda s, i, pick: (always[0], i % 2, 0, 0)
        return pl.BlockSpec((1, 2, left.shape[2], wide), index)

    def right_spec(which):
        if not both:
            index = (lambda s, i, pick: (i, 0, pick[s])) if which == alone else (lambda s, i, pick: (0, 0, 0))
        elif which == 0:
            index = lambda s, i, pick: (jnp.minimum(i, 1), 0, pick[s])
        else:
            index = lambda s, i, pick: (jnp.maximum(i - 2, 0), 0, pick[s])
        return pl.BlockSpec((2, count, columns), index)

    return pl.pallas_call(
        functools.partial(accumulate, low, steps),
        grid_spec=pltpu.PrefetchScalarGridSpec(
            num_scalar_prefetch=1,
            grid=(n, 4 if both else 2),
            in_specs=[left_spec(k, left) for k, left in enumerate(lefts)]
            + [right_spec(which) for which in range(ZLO)]
            + ([] if total is None else [block]),
            out_specs=block if n > 1 else pl.BlockSpec((1, wide, columns), lambda s, i, pick: (0, 0, 0)),
        ),
        out_shape=jax.ShapeDtypeStruct((n, wide, columns), jnp.float32),
        compiler_params=pltpu.CompilerParams(vmem_limit_bytes=56 * 2**20),
        cost_estimate=pl.CostEstimate(
            flops=6 * n * ZLO * X * rows * wide * columns,
            bytes_accessed=4 * n * ZLO * X * (rows + count) * wide,
            transcendentals=0,
        ),
    )(sides, *lefts, *panels, *(() if total is None else (total,)))


def body(jacobian, obs_group, group_weight, misfit):
    x, zlo, zhi, y, core = (lax.axis_index(name) for name in NAMES)
    count, columns = jacobian.shape[0] // CORE, jacobian.shape[1]
    levels = jnp.arange(group_weight.shape[0], dtype=jnp.int32)
    onehot = (obs_group[:, None] == levels[None, :]).astype(jnp.float32)
    weight_row = jnp.sum(onehot * group_weight[None, :], axis=1)
    names = "abcd"[: len(PHASES)]
    low = {p: sum(PHASES[: names.index(p)]) for p in names}
    size = dict(zip(names, PHASES))
    got = {}

    kept = lax.dynamic_slice_in_dim(jacobian, core * count, count, 0)
    given = lax.dynamic_slice_in_dim(jacobian, (1 - core) * count, count, 0)
    taken = send(given, flip_core)
    mine = jnp.where(
        core == 0, jnp.concatenate([kept, taken], 1), jnp.concatenate([taken, kept], 1)
    )
    row_weight = lax.dynamic_slice_in_dim(weight_row, core * count, count, 0)[:, None]
    row_misfit = lax.dynamic_slice_in_dim(misfit, core * count, count, 0)[:, None]
    local = jnp.sum(mine * (row_weight * row_misfit), axis=0)

    def weighted(p):
        rows = slice(low[p], low[p] + size[p])
        return mine[rows] * row_weight[rows]

    def wide():
        return jnp.concatenate([mine, jnp.broadcast_to(local[None], (TILE, 2 * columns))], 0)

    def partner():
        return got["Z"].at[count:].add(local[None])

    def both(*names):
        return jnp.concatenate([got[n] if got[n].ndim == 3 else got[n][None] for n in names], 0)

    rings = {"N": flip_y(NEAR), "F": flip_y(FAR)}
    moves = {
        "X1": (lambda: mine, flip_x(NEAR)),
        "X2": (lambda: jnp.stack([mine, got["X1"]]), flip_x(FAR)),
        "Z": (wide, flip_zlo),
        "V1": (partner, flip_x(NEAR)),
        "V2": (lambda: jnp.stack([partner(), got["V1"]]), flip_x(FAR)),
    }
    for p in size:
        moves["T1" + p] = (functools.partial(weighted, p), spread_yz)
        moves["T2" + p] = (lambda p=p: got["T1" + p], spread_x)
        moves["ZH" + p] = (lambda p=p: got["T2" + p], flip_zhi)
        moves["NO" + p] = (lambda p=p: got["T2" + p], rings["N"])
        moves["FO" + p] = (lambda p=p: both("T2" + p, "NO" + p), rings["F"])
        moves["NP" + p] = (lambda p=p: got["ZH" + p], rings["N"])
        moves["FP" + p] = (lambda p=p: both("ZH" + p, "NP" + p), rings["F"])
        moves["NC" + p] = (lambda p=p: both("T2" + p, "ZH" + p), rings["N"])
        moves["FC" + p] = (lambda p=p: both("T2" + p, "ZH" + p, "NC" + p), rings["F"])

    token = jnp.zeros((TILE, 128), jnp.float32)
    for name, *after in ORDER:
        value = moves[name][0]()
        if after:
            held = [got[a] for a in after]
            value, token, *held = lax.optimization_barrier((value, token, *held))
            got.update(zip(after, held))
        got[name] = send(value, moves[name][1])

    near = jnp.where(core == 0, NEAR[0], NEAR[1])
    far = jnp.where(core == 0, FAR[0], FAR[1])

    def panel(first, one, two):
        out = jnp.zeros((X, *first.shape), jnp.float32)
        for at, block in ((0, first), (near, one), (far, two[0]), (near ^ far, two[1])):
            out = lax.dynamic_update_slice(out, block[None], (at, 0, 0))
        return out

    panels = (
        panel(mine, got["X1"], got["X2"]),
        panel(partner(), got["V1"], got["V2"]),
    )
    slope = jnp.sum(panels[1][:, count], axis=0)
    gradient = lax.dynamic_slice_in_dim(slope, core * columns, columns, 0) + send(
        lax.dynamic_slice_in_dim(slope, (1 - core) * columns, columns, 0), flip_core
    )

    def collect(p):
        out = jnp.zeros((ZLO, X, size[p], 2 * columns), jnp.float32)
        for other in range(ZHI):
            if "NC" + p in got:
                k = other
                pieces = ((0, got["ZH" + p] if other else got["T2" + p]), (near, got["NC" + p][k]))
                pieces += ((far, got["FC" + p][k]), (near ^ far, got["FC" + p][2 + k]))
            else:
                first, one, two = (got[n + p] for n in (("ZH", "NP", "FP") if other else ("T2", "NO", "FO")))
                pieces = ((0, first), (near, one), (far, two[0]), (near ^ far, two[1]))
            for step, block in pieces:
                there = y ^ step
                at = 2 * (zhi ^ other ^ core) + ((there >> 1) ^ core)
                out = lax.dynamic_update_slice(out, block[None, None], (there & 1, at, 0, 0))
        return out

    sides = jnp.stack([1 - core, core]).astype(jnp.int32)
    *early, last = size
    blocks, rows = [collect(p) for p in size], [low[p] for p in size]
    total = product(blocks[:-1], rows[:-1], (panels[0], panels[0]), sides, None, [[0], []])
    final = functools.partial(product, blocks, rows, panels)
    theirs = final(sides[:1], total, [[1], [0, 1]])
    swapped = send(theirs[0], flip_core)
    ours = final(sides[1:], total, [[1], [0, 1]])
    return ours[0] + swapped, gradient + token[0, 0]


def solution(mesh):
    fine = Mesh(mesh.devices.reshape(SIZES), NAMES)
    return jax.shard_map(
        body,
        mesh=fine,
        in_specs=(P(("x", "zlo"), ("zhi", "y", "core")), P(("x", "zlo")), P(), P(("x", "zlo"))),
        out_specs=(P(("x", "zlo"), ("zhi", "y", "core")), P(("zhi", "y", "core"))),
        check_vma=False,
    )
```

time: 692 us -> 192 us (0.28)
  the two profiles are of different devices: /device:TPU:39 before, /device:TPU:3 now
where the time goes in v1:
time: 192 us; the launch traced here: 191 us
  starting transfers between devices  60.4 us (31%)
  Pallas kernels  44 us (23%)
  waiting for transfers between devices  41.3 us (22%)
  local copies, waits for them, and re-layouts  31.4 us (16%)
  other arithmetic  13.4 us (7%)
    ppermute x22, starting transfers between devices, send(): return lax.ppermute(value, NAMES, pairs)  60.4 us
    pallas_call x3, Pallas kernels, product(): pl.pallas_call(functools.partial(accumulate, low, steps), grid_spec=pltpu...  44 us
    ppermute x22, waiting for transfers between devices, send(): return lax.ppermute(value, NAMES, pairs)  41.3 us
    dynamic_update_slice x8, local copies, waits for them, and re-layouts, panel(): out = lax.dynamic_update_slice(out, block[None], (at, 0, 0))  13.9 us
    dynamic_update_slice x16, local copies, waits for them, and re-layouts, collect(): lax.dynamic_update_slice(out, block[None, None], (there & 1, at, 0, 0))  10.3 us
    add x2, other arithmetic, body(): return (ours[0] + swapped, gradient + token[0, 0])  5.32 us
  transfers between devices with their start and end apart: 22, of which 11 were waited for; matrix products, arithmetic and copies ran while one was open for 19% of the time, Pallas kernels for 15%

profile of v1, /device:TPU:3, one launch (start us, length us, event | category | flops | bytes accessed | tf_op | source)
XLA Modules:
  0.0 191.4 jit_solution(16059171239307356469)
XLA Ops:
  0.6 1.3 constant_dynamic-slice_fusion
  6.5 5.5 %collective-permute-start.1 = (f32[96,1280]{1,0:T(8,128)S(1)}, f32[96,1280]{1,0:T(8,128)S(1)}, u32[]{:S(2)}, u32[]{:S(2)}) collective-permute-start(f32[96,1280]{1,0:T(8,128)S(1)} %slice_multiply_fusion.1), channel_id=1, source_target_pairs={{0,0},{1,13},{2,18},{3,31},{4,4},{5,9},{6,22},{7,27},{8,8},{9,5},{... | collective-permute-start | bytes 1474568 | tf_op jit(solution)/shard_map/ppermute | solution.py:51
  12.1 2.4 %dynamic_update_slice.88 = f32[4,224,1280]{2,1,0:T(8,128)} pad(f32[1,224,1280]{2,1,0:T(8,128)S(1)} %maximum_select_fusion.1, f32[]{:T(128)} %constant.89.clone.1), padding=0_3x0_0x0_0 | pad | bytes 5734404 | tf_op jit(solution)/shard_map/dynamic_update_slice | solution.py:239
  14.6 3.6 %collective-permute-done.1 = f32[96,1280]{1,0:T(8,128)S(1)} collective-permute-done((f32[96,1280]{1,0:T(8,128)S(1)}, f32[96,1280]{1,0:T(8,128)S(1)}, u32[]{:S(2)}, u32[]{:S(2)}) %collective-permute-start.1) | collective-permute-done | bytes 491552 | tf_op jit(solution)/shard_map/ppermute | solution.py:51
  18.2 1.9 collective-permute-start.2
  20.2 8.8 %collective-permute-start.5 = (f32[128,1280]{1,0:T(8,128)S(1)}, f32[128,1280]{1,0:T(8,128)S(1)}, u32[]{:S(2)}, u32[]{:S(2)}) collective-permute-start(f32[128,1280]{1,0:T(8,128)S(1)} %slice_multiply_fusion), channel_id=1, source_target_pairs={{0,0},{1,13},{2,18},{3,31},{4,4},{5,9},{6,22},{7,27},{8,8},{9,5},{... | collective-permute-start | bytes 1966088 | tf_op jit(solution)/shard_map/ppermute | solution.py:51
  29.0 9.0 %collective-permute-start.6 = (f32[96,1280]{1,0:T(8,128)S(1)}, f32[96,1280]{1,0:T(8,128)S(1)}, u32[]{:S(2)}, u32[]{:S(2)}) collective-permute-start(f32[96,1280]{1,0:T(8,128)S(1)} %collective-permute-done.2), channel_id=1, source_target_pairs={{0,8},{1,9},{2,10},{3,11},{4,12},{5,13},{6,14},{7,15},{8,0},{9,1},... | collective-permute-start | bytes 1474568 | tf_op jit(solution)/shard_map/ppermute | solution.py:51
  38.3 2.2 %broadcast_in_dim.44 = f32[2,4,96,1280]{3,2,1,0:T(8,128)} broadcast(f32[]{:T(128)} %constant.89.clone.1), dimensions={} | broadcast | bytes 3932164 | tf_op jit(solution)/shard_map/broadcast_in_dim | solution.py:252
  41.4 2.9 %collective-permute-start.9 = (f32[128,1280]{1,0:T(8,128)S(1)}, f32[128,1280]{1,0:T(8,128)S(1)}, u32[]{:S(2)}, u32[]{:S(2)}) collective-permute-start(f32[128,1280]{1,0:T(8,128)S(1)} %collective-permute-done.5), channel_id=1, source_target_pairs={{0,0},{1,97},{2,2},{3,99},{4,36},{5,69},{6,38},{7,71},{8,72},{9,41... | collective-permute-start | bytes 1966088 | tf_op jit(solution)/shard_map/ppermute | solution.py:51
  47.3 2.1 %collective-permute-done.6 = f32[96,1280]{1,0:T(8,128)S(1)} collective-permute-done((f32[96,1280]{1,0:T(8,128)S(1)}, f32[96,1280]{1,0:T(8,128)S(1)}, u32[]{:S(2)}, u32[]{:S(2)}) %collective-permute-start.6) | collective-permute-done | bytes 491552 | tf_op jit(solution)/shard_map/ppermute | solution.py:51
  49.4 3.8 %collective-permute-start.7 = (f32[96,1280]{1,0:T(8,128)S(1)}, f32[96,1280]{1,0:T(8,128)S(1)}, u32[]{:S(2)}, u32[]{:S(2)}) collective-permute-start(f32[96,1280]{1,0:T(8,128)S(1)} %collective-permute-done.6), channel_id=1, source_target_pairs={{0,2},{1,7},{2,0},{3,5},{4,6},{5,3},{6,4},{7,1},{8,10},{9,15},{10,... | collective-permute-start | bytes 1474568 | tf_op jit(solution)/shard_map/ppermute | solution.py:51
  54.0 3.5 %collective-permute-done.9 = f32[128,1280]{1,0:T(8,128)S(1)} collective-permute-done((f32[128,1280]{1,0:T(8,128)S(1)}, f32[128,1280]{1,0:T(8,128)S(1)}, u32[]{:S(2)}, u32[]{:S(2)}) %collective-permute-start.9) | collective-permute-done | bytes 655392 | tf_op jit(solution)/shard_map/ppermute | solution.py:51
  57.5 5.8 %collective-permute-start.11 = (f32[128,1280]{1,0:T(8,128)S(1)}, f32[128,1280]{1,0:T(8,128)S(1)}, u32[]{:S(2)}, u32[]{:S(2)}) collective-permute-start(f32[128,1280]{1,0:T(8,128)S(1)} %collective-permute-done.9), channel_id=1, source_target_pairs={{0,2},{1,7},{2,0},{3,5},{4,6},{5,3},{6,4},{7,1},{8,10},{9,15},{10,... | collective-permute-start | bytes 1966088 | tf_op jit(solution)/shard_map/ppermute | solution.py:51
  64.0 9.7 %collective-permute-done.8 = f32[232,1280]{1,0:T(8,128)S(1)} collective-permute-done((f32[232,1280]{1,0:T(8,128)S(1)}, f32[232,1280]{1,0:T(8,128)S(1)}, u32[]{:S(2)}, u32[]{:S(2)}) %collective-permute-start.8) | collective-permute-done | bytes 1187872 | tf_op jit(solution)/shard_map/ppermute | solution.py:51
  74.1 2.4 %dynamic_update_slice.92 = f32[4,232,1280]{2,1,0:T(8,128)} pad(f32[1,232,1280]{2,1,0:T(8,128)S(1)} %bitcast_dynamic-update-slice_fusion.16, f32[]{:T(128)} %constant.89.clone.1), padding=0_3x0_0x0_0 | pad | bytes 5939204 | tf_op jit(solution)/shard_map/dynamic_update_slice | solution.py:239
  78.4 1.7 collective-permute-start.12
  83.4 8.5 %collective-permute-done.12 = f32[2,96,1280]{2,1,0:T(8,128)S(1)} collective-permute-done((f32[2,96,1280]{2,1,0:T(8,128)S(1)}, f32[2,96,1280]{2,1,0:T(8,128)S(1)}, u32[]{:S(2)}, u32[]{:S(2)}) %collective-permute-start.12) | collective-permute-done | bytes 983072 | tf_op jit(solution)/shard_map/ppermute | solution.py:51
  91.9 2.4 %collective-permute-start.16 = (f32[128,1280]{1,0:T(8,128)S(1)}, f32[128,1280]{1,0:T(8,128)}, u32[]{:S(2)}, u32[]{:S(2)}) collective-permute-start(f32[128,1280]{1,0:T(8,128)S(1)} %collective-permute-done.14), channel_id=1, source_target_pairs={{0,2},{1,7},{2,0},{3,5},{4,6},{5,3},{6,4},{7,1},{8,10},{9,15},{10,... | collective-permute-start | bytes 1966088 | tf_op jit(solution)/shard_map/ppermute | solution.py:51
  95.3 1.7 pad_maximum_fusion
  97.0 1.7 collective-permute-start.19
  102.6 12.6 %shard_map.59.refs_4_ = f32[2,1280,640]{2,1,0:T(8,128)} custom-call(s32[2]{0:T(128)} %pad_add_fusion.pick_ref, f32[2,4,96,1280]{3,2,1,0:T(8,128)} %bitcast_dynamic-update-slice_fusion.8.refs_0_, f32[4,224,1280]{2,1,0:T(8,128)} %slice_dynamic-update-slice_fusion.2.refs_1_.refs_2_, f32[4,224,1280]{2,1,0:T(8,128)} %slice_dynamic-update-slice_fusion.2.refs_1_.refs_2_), custom_call_target="tpu_custom_call" | custom-call | flops 7549747200 | bytes 26214400 | tf_op jit(solution)/shard_map/pallas_call | solution.py:151
  122.8 2.9 %collective-permute-done.19 = f32[2,232,1280]{2,1,0:T(8,128)} collective-permute-done((f32[2,232,1280]{2,1,0:T(8,128)}, f32[2,232,1280]{2,1,0:T(8,128)}, u32[]{:S(2)}, u32[]{:S(2)}) %collective-permute-start.19) | collective-permute-done | bytes 2375712 | tf_op jit(solution)/shard_map/ppermute | solution.py:51
  125.7 2.4 %slice_dynamic-update-slice_fusion.1 = f32[4,232,1280]{2,1,0:T(8,128)} fusion(f32[4,232,1280]{2,1,0:T(8,128)} %bitcast_dynamic-update-slice_fusion, s32[]{:T(128)S(6)} %select_n.115, f32[2,232,1280]{2,1,0:T(8,128)} %collective-permute-done.19), kind=kLoop, calls=%fused_computation.6 | loop fusion | bytes 2375684 | tf_op jit(solution)/shard_map/dynamic_update_slice | solution.py:239
  128.1 2.4 %slice_dynamic-update-slice_fusion.refs_3_ = f32[4,232,1280]{2,1,0:T(8,128)} fusion(f32[4,232,1280]{2,1,0:T(8,128)} %slice_dynamic-update-slice_fusion.1, s32[]{:T(128)S(6)} %select_n.124, f32[2,232,1280]{2,1,0:T(8,128)} %collective-permute-done.19), kind=kLoop, calls=%fused_computation.5 | loop fusion | bytes 2375684 | tf_op jit(solution)/shard_map/dynamic_update_slice | solution.py:239
  130.5 4.8 %collective-permute-done.18 = f32[2,128,1280]{2,1,0:T(8,128)S(1)} collective-permute-done((f32[2,128,1280]{2,1,0:T(8,128)S(1)}, f32[2,128,1280]{2,1,0:T(8,128)S(1)}, u32[]{:S(2)}, u32[]{:S(2)}) %collective-permute-start.18) | collective-permute-done | bytes 1310752 | tf_op jit(solution)/shard_map/ppermute | solution.py:51
  135.4 2.3 %copy-done = f32[2,4,128,1280]{3,2,1,0:T(8,128)} copy-done((f32[2,4,128,1280]{3,2,1,0:T(8,128)}, f32[2,4,128,1280]{3,2,1,0:T(8,128)S(1)}, u32[]{:S(2)}) %copy-start) | copy-done | bytes 5242904
  137.7 15.7 %shard_map.61 = f32[1,1280,640]{2,1,0:T(8,128)} custom-call(s32[1]{0:T(128)} %bitcast.33.pick_ref, f32[2,4,96,1280]{3,2,1,0:T(8,128)} %bitcast_dynamic-update-slice_fusion.8.refs_0_, f32[2,4,128,1280]{3,2,1,0:T(8,128)} %copy-done, f32[4,224,1280]{2,1,0:T(8,128)} %slice_dynamic-update-slice_fusion.2.refs_1_.refs_2_, ...), custom_call_target="tpu_custom_call" | custom-call | flops 8808038400 | bytes 18350080 | tf_op jit(solution)/shard_map/pallas_call | solution.py:151
  153.4 11.5 %collective-permute-start.20 = (f32[1280,640]{1,0:T(8,128)}, f32[1280,640]{1,0:T(8,128)S(1)}, u32[]{:S(2)}, u32[]{:S(2)}) collective-permute-start(f32[1280,640]{1,0:T(8,128)} %bitcast.73), channel_id=1, source_target_pairs={{0,1},{1,0},{2,3},{3,2},{4,5},{5,4},{6,7},{7,6},{8,9},{9,8},{10,11... | collective-permute-start | bytes 9830408 | tf_op jit(solution)/shard_map/ppermute | solution.py:51
  166.6 3.8 %collective-permute-done.21 = f32[640]{0:T(1024)S(1)} collective-permute-done((f32[640]{0:T(1024)S(1)}, f32[640]{0:T(1024)S(1)}, u32[]{:S(2)}, u32[]{:S(2)}) %collective-permute-start.21) | collective-permute-done | bytes 2592 | tf_op jit(solution)/shard_map/ppermute | solution.py:51
  170.4 1.4 add_add_fusion
  171.8 15.7 %shard_map.60 = f32[1,1280,640]{2,1,0:T(8,128)} custom-call(s32[1]{0:T(128)} %bitcast.pick_ref, f32[2,4,96,1280]{3,2,1,0:T(8,128)} %bitcast_dynamic-update-slice_fusion.8.refs_0_, f32[2,4,128,1280]{3,2,1,0:T(8,128)} %copy-done, f32[4,224,1280]{2,1,0:T(8,128)} %slice_dynamic-update-slice_fusion.2.refs_1_.refs_2_, ...), custom_call_target="tpu_custom_call" | custom-call | flops 8808038400 | bytes 18350080 | tf_op jit(solution)/shard_map/pallas_call | solution.py:151
  187.4 4.0 %bitcast_add_fusion = f32[1280,640]{1,0:T(8,128)} fusion(f32[1280,640]{1,0:T(8,128)S(1)} %collective-permute-done.20, f32[1,1280,640]{2,1,0:T(8,128)} %shard_map.60), kind=kLoop, calls=%fused_computation | loop fusion | flops 819200 | bytes 9830400 | tf_op jit(solution)/shard_map/add | solution.py:275
  (71 shorter events, 30.1 us)
Async XLA Ops:
  2.0 3.0 %collective-permute-start = (f32[224,640]{1,0:T(8,128)S(1)}, f32[224,640]{1,0:T(8,128)S(1)}, u32[]{:S(2)}, u32[]{:S(2)}) collective-permute-start(f32[224,640]{1,0:T(8,128)S(1)} %get-tuple-element.144), channel_id=1, source_target_pairs={{0,1},{1,0},{2,3},{3,2},{4,5},{5,4},{6,7},{7,6},{8,9},{9,8},{10,11... | collective-permute-start | bytes 1720328 | tf_op jit(solution)/shard_map/ppermute | solution.py:51
  5.1 23.9 %collective-permute-start.3 = (f32[224,1280]{1,0:T(8,128)S(1)}, f32[224,1280]{1,0:T(8,128)S(1)}, u32[]{:S(2)}, u32[]{:S(2)}) collective-permute-start(f32[224,1280]{1,0:T(8,128)S(1)} %get-tuple-element.141), channel_id=1, source_target_pairs={{0,32},{1,97},{2,34},{3,99},{4,36},{5,101},{6,38},{7,103},{8,40},{... | collective-permute-start | bytes 3440648 | tf_op jit(solution)/shard_map/ppermute | solution.py:51
  6.5 11.7 %collective-permute-start.1 = (f32[96,1280]{1,0:T(8,128)S(1)}, f32[96,1280]{1,0:T(8,128)S(1)}, u32[]{:S(2)}, u32[]{:S(2)}) collective-permute-start(f32[96,1280]{1,0:T(8,128)S(1)} %slice_multiply_fusion.1), channel_id=1, source_target_pairs={{0,0},{1,13},{2,18},{3,31},{4,4},{5,9},{6,22},{7,27},{8,8},{9,5},{... | collective-permute-start | bytes 1474568 | tf_op jit(solution)/shard_map/ppermute | solution.py:51
  18.2 10.8 %collective-permute-start.2 = (f32[96,1280]{1,0:T(8,128)S(1)}, f32[96,1280]{1,0:T(8,128)S(1)}, u32[]{:S(2)}, u32[]{:S(2)}) collective-permute-start(f32[96,1280]{1,0:T(8,128)S(1)} %collective-permute-done.1), channel_id=1, source_target_pairs={{0,0},{1,97},{2,2},{3,99},{4,36},{5,69},{6,38},{7,71},{8,72},{9,41... | collective-permute-start | bytes 1474568 | tf_op jit(solution)/shard_map/ppermute | solution.py:51
  20.2 21.2 %collective-permute-start.5 = (f32[128,1280]{1,0:T(8,128)S(1)}, f32[128,1280]{1,0:T(8,128)S(1)}, u32[]{:S(2)}, u32[]{:S(2)}) collective-permute-start(f32[128,1280]{1,0:T(8,128)S(1)} %slice_multiply_fusion), channel_id=1, source_target_pairs={{0,0},{1,13},{2,18},{3,31},{4,4},{5,9},{6,22},{7,27},{8,8},{9,5},{... | collective-permute-start | bytes 1966088 | tf_op jit(solution)/shard_map/ppermute | solution.py:51
  29.0 20.3 %collective-permute-start.6 = (f32[96,1280]{1,0:T(8,128)S(1)}, f32[96,1280]{1,0:T(8,128)S(1)}, u32[]{:S(2)}, u32[]{:S(2)}) collective-permute-start(f32[96,1280]{1,0:T(8,128)S(1)} %collective-permute-done.2), channel_id=1, source_target_pairs={{0,8},{1,9},{2,10},{3,11},{4,12},{5,13},{6,14},{7,15},{8,0},{9,1},... | collective-permute-start | bytes 1474568 | tf_op jit(solution)/shard_map/ppermute | solution.py:51
  38.1 9.2 %collective-permute-start.4 = (f32[96,1280]{1,0:T(8,128)S(1)}, f32[96,1280]{1,0:T(8,128)S(1)}, u32[]{:S(2)}, u32[]{:S(2)}) collective-permute-start(f32[96,1280]{1,0:T(8,128)S(1)} %collective-permute-done.2), channel_id=1, source_target_pairs={{0,2},{1,7},{2,0},{3,5},{4,6},{5,3},{6,4},{7,1},{8,10},{9,15},{10,... | collective-permute-start | bytes 1474568 | tf_op jit(solution)/shard_map/ppermute | solution.py:51
  38.1 35.7 %collective-permute-start.8 = (f32[232,1280]{1,0:T(8,128)S(1)}, f32[232,1280]{1,0:T(8,128)S(1)}, u32[]{:S(2)}, u32[]{:S(2)}) collective-permute-start(f32[232,1280]{1,0:T(8,128)S(1)} %pad_maximum_fusion.4), channel_id=1, source_target_pairs={{0,16},{1,17},{2,18},{3,19},{4,20},{5,21},{6,22},{7,23},{8,24},{9,... | collective-permute-start | bytes 3563528 | tf_op jit(solution)/shard_map/ppermute | solution.py:51
  41.4 16.1 %collective-permute-start.9 = (f32[128,1280]{1,0:T(8,128)S(1)}, f32[128,1280]{1,0:T(8,128)S(1)}, u32[]{:S(2)}, u32[]{:S(2)}) collective-permute-start(f32[128,1280]{1,0:T(8,128)S(1)} %collective-permute-done.5), channel_id=1, source_target_pairs={{0,0},{1,97},{2,2},{3,99},{4,36},{5,69},{6,38},{7,71},{8,72},{9,41... | collective-permute-start | bytes 1966088 | tf_op jit(solution)/shard_map/ppermute | solution.py:51
  44.3 39.1 %collective-permute-start.13 = (f32[2,224,1280]{2,1,0:T(8,128)S(1)}, f32[2,224,1280]{2,1,0:T(8,128)S(1)}, u32[]{:S(2)}, u32[]{:S(2)}) collective-permute-start(f32[2,224,1280]{2,1,0:T(8,128)S(1)} %pad_maximum_fusion.1), channel_id=1, source_target_pairs={{0,96},{1,33},{2,98},{3,35},{4,100},{5,37},{6,102},{7,39},{8,104},... | collective-permute-start | bytes 6881288 | tf_op jit(solution)/shard_map/ppermute | solution.py:51
  49.4 14.4 %collective-permute-start.7 = (f32[96,1280]{1,0:T(8,128)S(1)}, f32[96,1280]{1,0:T(8,128)S(1)}, u32[]{:S(2)}, u32[]{:S(2)}) collective-permute-start(f32[96,1280]{1,0:T(8,128)S(1)} %collective-permute-done.6), channel_id=1, source_target_pairs={{0,2},{1,7},{2,0},{3,5},{4,6},{5,3},{6,4},{7,1},{8,10},{9,15},{10,... | collective-permute-start | bytes 1474568 | tf_op jit(solution)/shard_map/ppermute | solution.py:51
  53.2 25.2 %collective-permute-start.10 = (f32[2,96,1280]{2,1,0:T(8,128)S(1)}, f32[2,96,1280]{2,1,0:T(8,128)S(1)}, u32[]{:S(2)}, u32[]{:S(2)}) collective-permute-start(f32[2,96,1280]{2,1,0:T(8,128)S(1)} %pad_maximum_fusion.5), channel_id=1, source_target_pairs={{0,6},{1,3},{2,4},{3,1},{4,2},{5,7},{6,0},{7,5},{8,14},{9,11},{10,... | collective-permute-start | bytes 2949128 | tf_op jit(solution)/shard_map/ppermute | solution.py:51
  57.5 19.7 %collective-permute-start.11 = (f32[128,1280]{1,0:T(8,128)S(1)}, f32[128,1280]{1,0:T(8,128)S(1)}, u32[]{:S(2)}, u32[]{:S(2)}) collective-permute-start(f32[128,1280]{1,0:T(8,128)S(1)} %collective-permute-done.9), channel_id=1, source_target_pairs={{0,2},{1,7},{2,0},{3,5},{4,6},{5,3},{6,4},{7,1},{8,10},{9,15},{10,... | collective-permute-start | bytes 1966088 | tf_op jit(solution)/shard_map/ppermute | solution.py:51
  63.8 28.0 %collective-permute-start.14 = (f32[128,1280]{1,0:T(8,128)S(1)}, f32[128,1280]{1,0:T(8,128)S(1)}, u32[]{:S(2)}, u32[]{:S(2)}) collective-permute-start(f32[128,1280]{1,0:T(8,128)S(1)} %collective-permute-done.9), channel_id=1, source_target_pairs={{0,8},{1,9},{2,10},{3,11},{4,12},{5,13},{6,14},{7,15},{8,0},{9,1},... | collective-permute-start | bytes 1966088 | tf_op jit(solution)/shard_map/ppermute | solution.py:51
  74.0 17.9 %collective-permute-start.15 = (f32[232,1280]{1,0:T(8,128)S(1)}, f32[232,1280]{1,0:T(8,128)S(1)}, u32[]{:S(2)}, u32[]{:S(2)}) collective-permute-start(f32[232,1280]{1,0:T(8,128)S(1)} %fusion.2), channel_id=1, source_target_pairs={{0,32},{1,97},{2,34},{3,99},{4,36},{5,101},{6,38},{7,103},{8,40},{... | collective-permute-start | bytes 3563528 | tf_op jit(solution)/shard_map/ppermute | solution.py:51
  78.4 13.5 %collective-permute-start.12 = (f32[2,96,1280]{2,1,0:T(8,128)S(1)}, f32[2,96,1280]{2,1,0:T(8,128)S(1)}, u32[]{:S(2)}, u32[]{:S(2)}) collective-permute-start(f32[2,96,1280]{2,1,0:T(8,128)S(1)} %pad_maximum_fusion.6), channel_id=1, source_target_pairs={{0,6},{1,3},{2,4},{3,1},{4,2},{5,7},{6,0},{7,5},{8,14},{9,11},{10,... | collective-permute-start | bytes 2949128 | tf_op jit(solution)/shard_map/ppermute | solution.py:51
  91.9 24.5 %collective-permute-start.16 = (f32[128,1280]{1,0:T(8,128)S(1)}, f32[128,1280]{1,0:T(8,128)}, u32[]{:S(2)}, u32[]{:S(2)}) collective-permute-start(f32[128,1280]{1,0:T(8,128)S(1)} %collective-permute-done.14), channel_id=1, source_target_pairs={{0,2},{1,7},{2,0},{3,5},{4,6},{5,3},{6,4},{7,1},{8,10},{9,15},{10,... | collective-permute-start | bytes 1966088 | tf_op jit(solution)/shard_map/ppermute | solution.py:51
  94.3 24.1 %collective-permute-start.17 = (f32[2,128,1280]{2,1,0:T(8,128)}, f32[2,128,1280]{2,1,0:T(8,128)}, u32[]{:S(2)}, u32[]{:S(2)}) collective-permute-start(f32[2,128,1280]{2,1,0:T(8,128)} %pad_maximum_fusion.2), channel_id=1, source_target_pairs={{0,6},{1,3},{2,4},{3,1},{4,2},{5,7},{6,0},{7,5},{8,14},{9,11},{10,... | collective-permute-start | bytes 3932168 | tf_op jit(solution)/shard_map/ppermute | solution.py:51
  97.0 28.8 %collective-permute-start.19 = (f32[2,232,1280]{2,1,0:T(8,128)}, f32[2,232,1280]{2,1,0:T(8,128)}, u32[]{:S(2)}, u32[]{:S(2)}) collective-permute-start(f32[2,232,1280]{2,1,0:T(8,128)} %pad_maximum_fusion), channel_id=1, source_target_pairs={{0,96},{1,33},{2,98},{3,35},{4,100},{5,37},{6,102},{7,39},{8,104},... | collective-permute-start | bytes 7127048 | tf_op jit(solution)/shard_map/ppermute | solution.py:51
  118.4 16.9 %collective-permute-start.18 = (f32[2,128,1280]{2,1,0:T(8,128)S(1)}, f32[2,128,1280]{2,1,0:T(8,128)S(1)}, u32[]{:S(2)}, u32[]{:S(2)}) collective-permute-start(f32[2,128,1280]{2,1,0:T(8,128)S(1)} %pad_maximum_fusion.3), channel_id=1, source_target_pairs={{0,6},{1,3},{2,4},{3,1},{4,2},{5,7},{6,0},{7,5},{8,14},{9,11},{10,... | collective-permute-start | bytes 3932168 | tf_op jit(solution)/shard_map/ppermute | solution.py:51
  135.4 2.3 %copy-start = (f32[2,4,128,1280]{3,2,1,0:T(8,128)}, f32[2,4,128,1280]{3,2,1,0:T(8,128)S(1)}, u32[]{:S(2)}) copy-start(f32[2,4,128,1280]{3,2,1,0:T(8,128)S(1)} %fusion.refs_1_) | copy-start | bytes 15728644
  153.4 34.0 %collective-permute-start.20 = (f32[1280,640]{1,0:T(8,128)}, f32[1280,640]{1,0:T(8,128)S(1)}, u32[]{:S(2)}, u32[]{:S(2)}) collective-permute-start(f32[1280,640]{1,0:T(8,128)} %bitcast.73), channel_id=1, source_target_pairs={{0,1},{1,0},{2,3},{3,2},{4,5},{5,4},{6,7},{7,6},{8,9},{9,8},{10,11... | collective-permute-start | bytes 9830408 | tf_op jit(solution)/shard_map/ppermute | solution.py:51
  165.9 4.5 %collective-permute-start.21 = (f32[640]{0:T(1024)S(1)}, f32[640]{0:T(1024)S(1)}, u32[]{:S(2)}, u32[]{:S(2)}) collective-permute-start(f32[640]{0:T(1024)S(1)} %dynamic_slice.23), channel_id=1, source_target_pairs={{0,1},{1,0},{2,3},{3,2},{4,5},{5,4},{6,7},{7,6},{8,9},{9,8},{10,11... | collective-permute-start | bytes 7688 | tf_op jit(solution)/shard_map/ppermute | solution.py:51

commit v2 on v1

--- a/solution.py
+++ b/solution.py
@@ -17,9 +17,9 @@
     ('T1a',),
     ('T2a', 'T1a'),
     ('T1b', 'T1a'),
-    ('Z', 'X1'),
     ('NOa', 'T2a'),
     ('ZHa', 'T2a'),
+    ('Z', 'X1'),
     ('T2b', 'T1b'),
     ('X2', 'X1'),
     ('FOa', 'NOa'),
@@ -98,74 +98,70 @@
     return dot(left_high, right_high) + (dot(left_low, right_high) + dot(left_high, right_low))
 
 
-def accumulate(low, steps, pick_ref, *refs):
-    lefts, rights = refs[: len(low)], refs[len(low) : len(low) + ZLO]
-    out_ref, rest = refs[-1], refs[len(low) + ZLO : -1]
+def accumulate(low, steps, based, pick_ref, *refs):
+    lefts, rights, outs = refs[: len(low)], refs[len(low) : len(low) + 2 * CORE * len(steps)], refs[-CORE:]
     step = pl.program_id(1)
-
-    @pl.when(step == 0)
-    def _():
-        out_ref[...] = rest[0][...] if rest else jnp.zeros_like(out_ref)
-
-    for which in range(ZLO):
-        if steps[which]:
-
-            @pl.when(step // 2 == which if all(steps) else step >= 0)
-            def _():
-                out_ref[0] += functools.reduce(
-                    lambda p, q: p + q,
-                    [
-                        contract(lefts[k][0], rights[which][:, low[k] : low[k] + lefts[k].shape[2]])
-                        for k in steps[which]
-                    ],
-                )
-
-
-def product(lefts, low, panels, sides, total, steps):
-    wide = panels[0].shape[-1]
-    columns = wide // CORE
-    count = panels[0].shape[1] // TILE * TILE
-    n = sides.shape[0]
-    block = pl.BlockSpec((1, wide, columns), lambda s, i, pick: (pick[s], 0, 0))
-    rows = sum(left.shape[2] for left in lefts)
-    both = all(steps)
-    alone = 0 if steps[0] else 1
+    columns = outs[0].shape[-1]
+
+    def add(i):
+        named = steps[i][0]
+        left = jnp.concatenate([lefts[k][0] for k in named], 1)
+        first, last = low[named[0]], low[named[-1]] + lefts[named[-1]].shape[2]
+        pairs = []
+        for pair in range(2):
+            at = 2 * CORE * i + CORE * pair
+            pairs.append(jnp.concatenate([rights[at + side][:, first:last] for side in range(CORE)], 2))
+        term = contract(left, jnp.concatenate(pairs, 0))
+        for side, out_ref in enumerate(outs):
+            part = term[:, side * columns : (side + 1) * columns]
+            if based and i == 0:
+                part = part + refs[len(low) + 2 * CORE * len(steps) + side][...]
+            out_ref[...] = part if i == 0 else out_ref[...] + part
+
+    for i in range(len(steps)):
+        pl.when(step == i)(functools.partial(add, i))
+
+
+def product(lefts, low, rights, sides, steps, base=()):
+    columns = rights[0].shape[-1] // CORE
+    rows, many = sum(left.shape[2] for left in lefts), len(steps)
 
     def left_spec(k, left):
-        always = [which for which in range(ZLO) if k in steps[which]]
-        if len(always) == 2:
-            index = lambda s, i, pick: (i // 2, i % 2, 0, 0)
-        else:
-            index = lambda s, i, pick: (always[0], i % 2, 0, 0)
-        return pl.BlockSpec((1, 2, left.shape[2], wide), index)
-
-    def right_spec(which):
-        if not both:
-            index = (lambda s, i, pick: (i, 0, pick[s])) if which == alone else (lambda s, i, pick: (0, 0, 0))
-        elif which == 0:
-            index = lambda s, i, pick: (jnp.minimum(i, 1), 0, pick[s])
-        else:
-            index = lambda s, i, pick: (jnp.maximum(i - 2, 0), 0, pick[s])
-        return pl.BlockSpec((2, count, columns), index)
-
+        first = min(z for named, z in steps if k in named)
+        return pl.BlockSpec(
+            (1, X, left.shape[2], columns), lambda h, i, pick: (jnp.maximum(i, first), 0, 0, h)
+        )
+
+    def right_spec(right, side):
+        return pl.BlockSpec((2, right.shape[1], columns), lambda h, i, pick: (0, 0, pick[side]))
+
+    half = pl.BlockSpec((columns, columns), lambda h, i, pick: (h, 0))
     return pl.pallas_call(
-        functools.partial(accumulate, low, steps),
+        functools.partial(accumulate, low, steps, len(base) > 0),
         grid_spec=pltpu.PrefetchScalarGridSpec(
             num_scalar_prefetch=1,
-            grid=(n, 4 if both else 2),
+            grid=(CORE, many),
             in_specs=[left_spec(k, left) for k, left in enumerate(lefts)]
-            + [right_spec(which) for which in range(ZLO)]
-            + ([] if total is None else [block]),
-            out_specs=block if n > 1 else pl.BlockSpec((1, wide, columns), lambda s, i, pick: (0, 0, 0)),
+            + [right_spec(right, side) for right in rights for side in range(CORE)]
+            + [half] * len(base),
+            out_specs=[half] * CORE,
         ),
-        out_shape=jax.ShapeDtypeStruct((n, wide, columns), jnp.float32),
-        compiler_params=pltpu.CompilerParams(vmem_limit_bytes=56 * 2**20),
+        out_shape=[jax.ShapeDtypeStruct((CORE * columns, columns), jnp.float32)] * CORE,
+        compiler_params=pltpu.CompilerParams(vmem_limit_bytes=61 * 2**20),
         cost_estimate=pl.CostEstimate(
-            flops=6 * n * ZLO * X * rows * wide * columns,
-            bytes_accessed=4 * n * ZLO * X * (rows + count) * wide,
+            flops=48 * many * rows * CORE * columns * columns,
+            bytes_accessed=64 * many * rows * columns,
             transcendentals=0,
         ),
-    )(sides, *lefts, *panels, *(() if total is None else (total,)))
+    )(sides, *lefts, *(right for right in rights for _ in range(CORE)), *base)
+
+
+def place(buffer, shape, blocks):
+    out = jnp.zeros(shape, jnp.float32) if buffer is None else buffer
+    for array, index, one, two in blocks:
+        block = array if index is None else array[index]
+        out = lax.dynamic_update_slice(out, block[None, None, : shape[2]], (one, two, 0, 0))
+    return out
 
 
 def body(jacobian, obs_group, group_weight, misfit):
@@ -177,7 +173,8 @@
     names = "abcd"[: len(PHASES)]
     low = {p: sum(PHASES[: names.index(p)]) for p in names}
     size = dict(zip(names, PHASES))
-    got = {}
+    names_last = names[-1]
+    got, sent = {}, {}
 
     kept = lax.dynamic_slice_in_dim(jacobian, core * count, count, 0)
     given = lax.dynamic_slice_in_dim(jacobian, (1 - core) * count, count, 0)
@@ -228,51 +225,40 @@
             held = [got[a] for a in after]
             value, token, *held = lax.optimization_barrier((value, token, *held))
             got.update(zip(after, held))
+        sent[name] = value
         got[name] = send(value, moves[name][1])
 
     near = jnp.where(core == 0, NEAR[0], NEAR[1])
     far = jnp.where(core == 0, FAR[0], FAR[1])
 
-    def panel(first, one, two):
-        out = jnp.zeros((X, *first.shape), jnp.float32)
-        for at, block in ((0, first), (near, one), (far, two[0]), (near ^ far, two[1])):
-            out = lax.dynamic_update_slice(out, block[None], (at, 0, 0))
-        return out
-
-    panels = (
-        panel(mine, got["X1"], got["X2"]),
-        panel(partner(), got["V1"], got["V2"]),
-    )
-    slope = jnp.sum(panels[1][:, count], axis=0)
+    slope = sent["V1"][count] + got["V1"][count] + got["V2"][0, count] + got["V2"][1, count]
     gradient = lax.dynamic_slice_in_dim(slope, core * columns, columns, 0) + send(
         lax.dynamic_slice_in_dim(slope, (1 - core) * columns, columns, 0), flip_core
     )
 
     def collect(p):
-        out = jnp.zeros((ZLO, X, size[p], 2 * columns), jnp.float32)
-        for other in range(ZHI):
-            if "NC" + p in got:
-                k = other
-                pieces = ((0, got["ZH" + p] if other else got["T2" + p]), (near, got["NC" + p][k]))
-                pieces += ((far, got["FC" + p][k]), (near ^ far, got["FC" + p][2 + k]))
-            else:
-                first, one, two = (got[n + p] for n in (("ZH", "NP", "FP") if other else ("T2", "NO", "FO")))
-                pieces = ((0, first), (near, one), (far, two[0]), (near ^ far, two[1]))
-            for step, block in pieces:
+        shape = (ZLO, X, size[p], 2 * columns)
+        out = None
+        for other, names in enumerate((("T2", "NO", "FO"), ("ZH", "NP", "FP"))):
+            first, one, two = (got[n + p] for n in names)
+            blocks = []
+            for step, array, index in ((0, first, None), (near, one, None), (far, two, 0), (near ^ far, two, 1)):
                 there = y ^ step
-                at = 2 * (zhi ^ other ^ core) + ((there >> 1) ^ core)
-                out = lax.dynamic_update_slice(out, block[None, None], (there & 1, at, 0, 0))
+                high = zhi ^ other ^ core
+                mixed = high ^ (there >> 1) ^ core
+                blocks.append((array, index, there & 1, jnp.where(core == 0, 2 * high + mixed, 2 * mixed + high)))
+            out = place(out, shape, blocks)
         return out
 
     sides = jnp.stack([1 - core, core]).astype(jnp.int32)
-    *early, last = size
-    blocks, rows = [collect(p) for p in size], [low[p] for p in size]
-    total = product(blocks[:-1], rows[:-1], (panels[0], panels[0]), sides, None, [[0], []])
-    final = functools.partial(product, blocks, rows, panels)
-    theirs = final(sides[:1], total, [[1], [0, 1]])
-    swapped = send(theirs[0], flip_core)
-    ours = final(sides[1:], total, [[1], [0, 1]])
-    return ours[0] + swapped, gradient + token[0, 0]
+    sides, token, got["NPb"] = lax.optimization_barrier((sides, token, got["NPb"]))
+    rows = [low[p] for p in size]
+    first, late = collect("a"), collect("b")
+    base = product([first], rows[:1], [sent["X2"], got["X2"]], sides, [([0], 0)])
+    rights = [sent["X2"], got["X2"], sent["V2"], got["V2"]]
+    steps = [([1], 0), ([0, 1], 1)]
+    theirs, ours = product([first, late], rows, rights, sides, steps, base)
+    return ours + send(theirs, flip_core), gradient + token[0, 0]
 
 
 def solution(mesh):

time: 192 us -> 177 us (0.922)
  the two profiles are of different devices: /device:TPU:3 before, /device:TPU:39 now
where the time goes in v2:
time: 177 us; the launch traced here: 174 us
  waiting for transfers between devices  67.8 us (38%)
  starting transfers between devices  43.5 us (25%)
  Pallas kernels  35.2 us (20%)
  local copies, waits for them, and re-layouts  16.7 us (9%)
  other arithmetic  9.83 us (6%)
    ppermute x22, waiting for transfers between devices, send(): return lax.ppermute(value, NAMES, pairs)  67.8 us
    ppermute x22, starting transfers between devices, send(): return lax.ppermute(value, NAMES, pairs)  43.5 us
    pallas_call x2, Pallas kernels, product(): pl.pallas_call(functools.partial(accumulate, low, steps, len(base) > 0),...  35.2 us
    dynamic_update_slice x16, local copies, waits for them, and re-layouts, place(): lax.dynamic_update_slice(out, block[None, None, :shape[2]], (one, two, 0,...  9.66 us
    add x2, other arithmetic, body(): return (ours + send(theirs, flip_core), gradient + token[0, 0])  5.28 us
  transfers between devices with their start and end apart: 22, of which 13 were waited for; matrix products, arithmetic and copies ran while one was open for 12% of the time, Pallas kernels for 6%

profile of v2, /device:TPU:39, one launch (start us, length us, event | category | flops | bytes accessed | tf_op | source)
XLA Modules:
  0.0 174.0 jit_solution(8588877490393996840)
XLA Ops:
  0.7 1.3 constant_dynamic-slice_fusion
  4.9 2.7 %collective-permute-start.1 = (f32[96,1280]{1,0:T(8,128)S(1)}, f32[96,1280]{1,0:T(8,128)S(1)}, u32[]{:S(2)}, u32[]{:S(2)}) collective-permute-start(f32[96,1280]{1,0:T(8,128)S(1)} %slice_multiply_fusion.1), channel_id=1, source_target_pairs={{0,0},{1,13},{2,18},{3,31},{4,4},{5,9},{6,22},{7,27},{8,8},{9,5},{... | collective-permute-start | bytes 1474568 | tf_op jit(solution)/shard_map/ppermute | solution.py:51
  7.9 6.9 %collective-permute-done.1 = f32[96,1280]{1,0:T(8,128)S(1)} collective-permute-done((f32[96,1280]{1,0:T(8,128)S(1)}, f32[96,1280]{1,0:T(8,128)S(1)}, u32[]{:S(2)}, u32[]{:S(2)}) %collective-permute-start.1) | collective-permute-done | bytes 491552 | tf_op jit(solution)/shard_map/ppermute | solution.py:51
  14.8 7.8 %collective-permute-start.3 = (f32[96,1280]{1,0:T(8,128)S(1)}, f32[96,1280]{1,0:T(8,128)S(1)}, u32[]{:S(2)}, u32[]{:S(2)}) collective-permute-start(f32[96,1280]{1,0:T(8,128)S(1)} %collective-permute-done.1), channel_id=1, source_target_pairs={{0,0},{1,97},{2,2},{3,99},{4,36},{5,69},{6,38},{7,71},{8,72},{9,41... | collective-permute-start | bytes 1474568 | tf_op jit(solution)/shard_map/ppermute | solution.py:51
  22.7 2.6 %collective-permute-start.2 = (f32[128,1280]{1,0:T(8,128)S(1)}, f32[128,1280]{1,0:T(8,128)S(1)}, u32[]{:S(2)}, u32[]{:S(2)}) collective-permute-start(f32[128,1280]{1,0:T(8,128)S(1)} %slice_multiply_fusion), channel_id=1, source_target_pairs={{0,0},{1,13},{2,18},{3,31},{4,4},{5,9},{6,22},{7,27},{8,8},{9,5},{... | collective-permute-start | bytes 1966088 | tf_op jit(solution)/shard_map/ppermute | solution.py:51
  25.3 3.4 %collective-permute-done.3 = f32[96,1280]{1,0:T(8,128)S(1)} collective-permute-done((f32[96,1280]{1,0:T(8,128)S(1)}, f32[96,1280]{1,0:T(8,128)S(1)}, u32[]{:S(2)}, u32[]{:S(2)}) %collective-permute-start.3) | collective-permute-done | bytes 491552 | tf_op jit(solution)/shard_map/ppermute | solution.py:51
  28.8 2.0 %collective-permute-start.6 = (f32[96,1280]{1,0:T(8,128)S(1)}, f32[96,1280]{1,0:T(8,128)S(1)}, u32[]{:S(2)}, u32[]{:S(2)}) collective-permute-start(f32[96,1280]{1,0:T(8,128)S(1)} %collective-permute-done.3), channel_id=1, source_target_pairs={{0,8},{1,9},{2,10},{3,11},{4,12},{5,13},{6,14},{7,15},{8,0},{9,1},... | collective-permute-start | bytes 1474568 | tf_op jit(solution)/shard_map/ppermute | solution.py:51
  30.8 1.0 collective-permute-start.7
  32.1 2.9 %collective-permute-start.11 = (f32[232,1280]{1,0:T(8,128)S(1)}, f32[232,1280]{1,0:T(8,128)S(1)}, u32[]{:S(2)}, u32[]{:S(2)}) collective-permute-start(f32[232,1280]{1,0:T(8,128)S(1)} %pad_maximum_fusion.4), channel_id=1, source_target_pairs={{0,16},{1,17},{2,18},{3,19},{4,20},{5,21},{6,22},{7,23},{8,24},{9,... | collective-permute-start | bytes 3563528 | tf_op jit(solution)/shard_map/ppermute | solution.py:51
  35.4 5.5 %collective-permute-start.5 = (f32[128,1280]{1,0:T(8,128)S(1)}, f32[128,1280]{1,0:T(8,128)S(1)}, u32[]{:S(2)}, u32[]{:S(2)}) collective-permute-start(f32[128,1280]{1,0:T(8,128)S(1)} %collective-permute-done.2), channel_id=1, source_target_pairs={{0,0},{1,97},{2,2},{3,99},{4,36},{5,69},{6,38},{7,71},{8,72},{9,41... | collective-permute-start | bytes 1966088 | tf_op jit(solution)/shard_map/ppermute | solution.py:51
  40.9 2.2 %collective-permute-done.7 = f32[96,1280]{1,0:T(8,128)S(1)} collective-permute-done((f32[96,1280]{1,0:T(8,128)S(1)}, f32[96,1280]{1,0:T(8,128)S(1)}, u32[]{:S(2)}, u32[]{:S(2)}) %collective-permute-start.7) | collective-permute-done | bytes 491552 | tf_op jit(solution)/shard_map/ppermute | solution.py:51
  43.2 2.9 %collective-permute-done.6 = f32[96,1280]{1,0:T(8,128)S(1)} collective-permute-done((f32[96,1280]{1,0:T(8,128)S(1)}, f32[96,1280]{1,0:T(8,128)S(1)}, u32[]{:S(2)}, u32[]{:S(2)}) %collective-permute-start.6) | collective-permute-done | bytes 491552 | tf_op jit(solution)/shard_map/ppermute | solution.py:51
  46.1 1.5 collective-permute-start.10
  47.9 6.1 %collective-permute-done.5 = f32[128,1280]{1,0:T(8,128)S(1)} collective-permute-done((f32[128,1280]{1,0:T(8,128)S(1)}, f32[128,1280]{1,0:T(8,128)S(1)}, u32[]{:S(2)}, u32[]{:S(2)}) %collective-permute-start.5) | collective-permute-done | bytes 655392 | tf_op jit(solution)/shard_map/ppermute | solution.py:51
  54.0 4.0 %collective-permute-start.9 = (f32[128,1280]{1,0:T(8,128)S(1)}, f32[128,1280]{1,0:T(8,128)S(1)}, u32[]{:S(2)}, u32[]{:S(2)}) collective-permute-start(f32[128,1280]{1,0:T(8,128)S(1)} %collective-permute-done.5), channel_id=1, source_target_pairs={{0,2},{1,7},{2,0},{3,5},{4,6},{5,3},{6,4},{7,1},{8,10},{9,15},{10,... | collective-permute-start | bytes 1966088 | tf_op jit(solution)/shard_map/ppermute | solution.py:51
  58.0 2.8 %broadcast_in_dim.91 = f32[2,4,128,1280]{3,2,1,0:T(8,128)} broadcast(f32[]{:T(128)} %constant.76.clone.1), dimensions={} | broadcast | bytes 5242884 | tf_op jit(solution)/shard_map/broadcast_in_dim | solution.py:160
  61.8 11.0 %collective-permute-done.11 = f32[232,1280]{1,0:T(8,128)S(1)} collective-permute-done((f32[232,1280]{1,0:T(8,128)S(1)}, f32[232,1280]{1,0:T(8,128)S(1)}, u32[]{:S(2)}, u32[]{:S(2)}) %collective-permute-start.11) | collective-permute-done | bytes 1187872 | tf_op jit(solution)/shard_map/ppermute | solution.py:51
  72.9 1.8 %collective-permute-start.15 = (f32[232,1280]{1,0:T(8,128)S(1)}, f32[232,1280]{1,0:T(8,128)S(1)}, u32[]{:S(2)}, u32[]{:S(2)}) collective-permute-start(f32[232,1280]{1,0:T(8,128)S(1)} %fusion.2), channel_id=1, source_target_pairs={{0,32},{1,97},{2,34},{3,99},{4,36},{5,101},{6,38},{7,103},{8,40},{... | collective-permute-start | bytes 3563528 | tf_op jit(solution)/shard_map/ppermute | solution.py:51
  75.1 13.0 %collective-permute-done.13 = f32[2,96,1280]{2,1,0:T(8,128)S(1)} collective-permute-done((f32[2,96,1280]{2,1,0:T(8,128)S(1)}, f32[2,96,1280]{2,1,0:T(8,128)S(1)}, u32[]{:S(2)}, u32[]{:S(2)}) %collective-permute-start.13) | collective-permute-done | bytes 983072 | tf_op jit(solution)/shard_map/ppermute | solution.py:51
  89.7 3.2 %collective-permute-start.16 = (f32[128,1280]{1,0:T(8,128)S(1)}, f32[128,1280]{1,0:T(8,128)S(1)}, u32[]{:S(2)}, u32[]{:S(2)}) collective-permute-start(f32[128,1280]{1,0:T(8,128)S(1)} %collective-permute-done.8), channel_id=1, source_target_pairs={{0,2},{1,7},{2,0},{3,5},{4,6},{5,3},{6,4},{7,1},{8,10},{9,15},{10,... | collective-permute-start | bytes 1966088 | tf_op jit(solution)/shard_map/ppermute | solution.py:51
  93.0 1.7 %pad_maximum_fusion.refs_6_.refs_7_ = f32[2,232,1280]{2,1,0:T(8,128)} fusion(f32[1,232,1280]{2,1,0:T(8,128)S(1)} %bitcast.65, f32[1,232,1280]{2,1,0:T(8,128)S(1)} %bitcast_dynamic-update-slice_fusion.14), kind=kLoop, calls=%fused_computation | loop fusion | flops 593920 | bytes 4751360 | tf_op jit(solution)/shard_map/stack | solution.py:208
  95.7 9.8 %collective-permute-done.16 = f32[128,1280]{1,0:T(8,128)S(1)} collective-permute-done((f32[128,1280]{1,0:T(8,128)S(1)}, f32[128,1280]{1,0:T(8,128)S(1)}, u32[]{:S(2)}, u32[]{:S(2)}) %collective-permute-start.16) | collective-permute-done | bytes 655392 | tf_op jit(solution)/shard_map/ppermute | solution.py:51
  105.5 5.5 %collective-permute-done.17 = f32[2,128,1280]{2,1,0:T(8,128)S(1)} collective-permute-done((f32[2,128,1280]{2,1,0:T(8,128)S(1)}, f32[2,128,1280]{2,1,0:T(8,128)S(1)}, u32[]{:S(2)}, u32[]{:S(2)}) %collective-permute-start.17) | collective-permute-done | bytes 1310752 | tf_op jit(solution)/shard_map/ppermute | solution.py:51
  113.1 10.4 %shard_map.59 = (f32[1280,640]{1,0:T(8,128)}, f32[1280,640]{1,0:T(8,128)}) custom-call(s32[2]{0:T(128)} %pad_add_fusion.pick_ref, f32[2,4,96,1280]{3,2,1,0:T(8,128)} %copy-done, f32[2,224,1280]{2,1,0:T(8,128)} %copy-done.1, f32[2,224,1280]{2,1,0:T(8,128)} %copy-done.1, f32[2,224,1280]{2,1,0:T(8,128)} %copy-done.7, f32[2,224,1280]{2,1,0:T(8,128)} %copy-done.7), custom_call_target="tpu_custom_call" | custom-call | flops 3774873600 | bytes 3932160 | tf_op jit(solution)/shard_map/pallas_call | solution.py:139
  125.2 2.6 %collective-permute-done.18 = f32[2,128,1280]{2,1,0:T(8,128)} collective-permute-done((f32[2,128,1280]{2,1,0:T(8,128)S(1)}, f32[2,128,1280]{2,1,0:T(8,128)}, u32[]{:S(2)}, u32[]{:S(2)}) %collective-permute-start.18) | collective-permute-done | bytes 1310752 | tf_op jit(solution)/shard_map/ppermute | solution.py:51
  127.9 2.0 %fusion.1 = f32[2,4,128,1280]{3,2,1,0:T(8,128)} fusion(f32[2,4,128,1280]{3,2,1,0:T(8,128)} %bitcast_dynamic-update-slice_fusion, s32[]{:T(128)S(6)} %select_n.143, s32[]{:T(128)S(6)} %select_n.154, f32[2,128,1280]{2,1,0:T(8,128)} %collective-permute-done.18), kind=kLoop, calls=%fused_computation.13 | loop fusion | bytes 1310728 | tf_op jit(solution)/shard_map/dynamic_update_slice | solution.py:163
  129.8 2.0 %fusion.refs_1_ = f32[2,4,128,1280]{3,2,1,0:T(8,128)} fusion(f32[2,4,128,1280]{3,2,1,0:T(8,128)} %fusion.1, s32[]{:T(128)S(6)} %select_n.146, s32[]{:T(128)S(6)} %select_n.156, f32[2,128,1280]{2,1,0:T(8,128)} %collective-permute-done.18), kind=kLoop, calls=%fused_computation.11 | loop fusion | bytes 1310728 | tf_op jit(solution)/shard_map/dynamic_update_slice | solution.py:163
  131.8 24.8 %shard_map.60 = (f32[1280,640]{1,0:T(8,128)}, f32[1280,640]{1,0:T(8,128)}) custom-call(s32[2]{0:T(128)} %pad_add_fusion.pick_ref, f32[2,4,96,1280]{3,2,1,0:T(8,128)} %copy-done, f32[2,4,128,1280]{3,2,1,0:T(8,128)} %fusion.refs_1_, f32[2,224,1280]{2,1,0:T(8,128)} %copy-done.1, f32[2,224,1280]{2,1,0:T(8,128)} %copy-done.1, f32[2,224,1280]{2,1,0:T(8,128)} %copy-done.7, ...), custom_call_target="tpu_custom_call" | custom-call | flops 17616076800 | bytes 18350080 | tf_op jit(solution)/shard_map/pallas_call | solution.py:139
  156.6 6.6 %collective-permute-start.20 = (f32[1280,640]{1,0:T(8,128)}, f32[1280,640]{1,0:T(8,128)S(1)}, u32[]{:S(2)}, u32[]{:S(2)}) collective-permute-start(f32[1280,640]{1,0:T(8,128)} %get-tuple-element.141), channel_id=1, source_target_pairs={{0,1},{1,0},{2,3},{3,2},{4,5},{5,4},{6,7},{7,6},{8,9},{9,8},{10,11... | collective-permute-start | bytes 9830408 | tf_op jit(solution)/shard_map/ppermute | solution.py:51
  165.6 3.2 %collective-permute-done.21 = f32[640]{0:T(1024)S(1)} collective-permute-done((f32[640]{0:T(1024)S(1)}, f32[640]{0:T(1024)S(1)}, u32[]{:S(2)}, u32[]{:S(2)}) %collective-permute-start.21) | collective-permute-done | bytes 2592 | tf_op jit(solution)/shard_map/ppermute | solution.py:51
  168.8 1.3 add_add_fusion.1
  170.1 4.0 %add.204 = f32[1280,640]{1,0:T(8,128)} add(f32[1280,640]{1,0:T(8,128)} %get-tuple-element.140, f32[1280,640]{1,0:T(8,128)S(1)} %collective-permute-done.20) | non-fusion elementwise | flops 819200 | bytes 9830400 | tf_op jit(solution)/shard_map/add | solution.py:261
  (78 shorter events, 14.5 us)
Async XLA Ops:
  0.6 2.1 %copy-start.5 = (f32[3]{0:T(128)S(1)}, f32[3]{0:T(128)}, u32[]{:S(2)}) copy-start(f32[3]{0:T(128)} %param.10) | copy-start | bytes 40
  0.6 2.1 %copy-start.4 = (s32[448]{0:T(512)S(1)}, s32[448]{0:T(512)}, u32[]{:S(2)}) copy-start(s32[448]{0:T(512)} %param.9) | copy-start | bytes 5380
  0.7 2.2 %copy-start.6 = (f32[448]{0:T(512)S(1)}, f32[448]{0:T(512)}, u32[]{:S(2)}) copy-start(f32[448]{0:T(512)} %param.11) | copy-start | bytes 5380
  2.0 2.4 %collective-permute-start = (f32[224,640]{1,0:T(8,128)S(1)}, f32[224,640]{1,0:T(8,128)S(1)}, u32[]{:S(2)}, u32[]{:S(2)}) collective-permute-start(f32[224,640]{1,0:T(8,128)S(1)} %get-tuple-element.150), channel_id=1, source_target_pairs={{0,1},{1,0},{2,3},{3,2},{4,5},{5,4},{6,7},{7,6},{8,9},{9,8},{10,11... | collective-permute-start | bytes 1720328 | tf_op jit(solution)/shard_map/ppermute | solution.py:51
  4.5 27.6 %collective-permute-start.4 = (f32[224,1280]{1,0:T(8,128)S(1)}, f32[224,1280]{1,0:T(8,128)S(1)}, u32[]{:S(2)}, u32[]{:S(2)}) collective-permute-start(f32[224,1280]{1,0:T(8,128)S(1)} %get-tuple-element.147), channel_id=1, source_target_pairs={{0,32},{1,97},{2,34},{3,99},{4,36},{5,101},{6,38},{7,103},{8,40},{... | collective-permute-start | bytes 3440648 | tf_op jit(solution)/shard_map/ppermute | solution.py:51
  4.9 9.9 %collective-permute-start.1 = (f32[96,1280]{1,0:T(8,128)S(1)}, f32[96,1280]{1,0:T(8,128)S(1)}, u32[]{:S(2)}, u32[]{:S(2)}) collective-permute-start(f32[96,1280]{1,0:T(8,128)S(1)} %slice_multiply_fusion.1), channel_id=1, source_target_pairs={{0,0},{1,13},{2,18},{3,31},{4,4},{5,9},{6,22},{7,27},{8,8},{9,5},{... | collective-permute-start | bytes 1474568 | tf_op jit(solution)/shard_map/ppermute | solution.py:51
  14.8 14.0 %collective-permute-start.3 = (f32[96,1280]{1,0:T(8,128)S(1)}, f32[96,1280]{1,0:T(8,128)S(1)}, u32[]{:S(2)}, u32[]{:S(2)}) collective-permute-start(f32[96,1280]{1,0:T(8,128)S(1)} %collective-permute-done.1), channel_id=1, source_target_pairs={{0,0},{1,97},{2,2},{3,99},{4,36},{5,69},{6,38},{7,71},{8,72},{9,41... | collective-permute-start | bytes 1474568 | tf_op jit(solution)/shard_map/ppermute | solution.py:51
  22.7 12.7 %collective-permute-start.2 = (f32[128,1280]{1,0:T(8,128)S(1)}, f32[128,1280]{1,0:T(8,128)S(1)}, u32[]{:S(2)}, u32[]{:S(2)}) collective-permute-start(f32[128,1280]{1,0:T(8,128)S(1)} %slice_multiply_fusion), channel_id=1, source_target_pairs={{0,0},{1,13},{2,18},{3,31},{4,4},{5,9},{6,22},{7,27},{8,8},{9,5},{... | collective-permute-start | bytes 1966088 | tf_op jit(solution)/shard_map/ppermute | solution.py:51
  28.8 17.3 %collective-permute-start.6 = (f32[96,1280]{1,0:T(8,128)S(1)}, f32[96,1280]{1,0:T(8,128)S(1)}, u32[]{:S(2)}, u32[]{:S(2)}) collective-permute-start(f32[96,1280]{1,0:T(8,128)S(1)} %collective-permute-done.3), channel_id=1, source_target_pairs={{0,8},{1,9},{2,10},{3,11},{4,12},{5,13},{6,14},{7,15},{8,0},{9,1},... | collective-permute-start | bytes 1474568 | tf_op jit(solution)/shard_map/ppermute | solution.py:51
  30.8 12.3 %collective-permute-start.7 = (f32[96,1280]{1,0:T(8,128)S(1)}, f32[96,1280]{1,0:T(8,128)S(1)}, u32[]{:S(2)}, u32[]{:S(2)}) collective-permute-start(f32[96,1280]{1,0:T(8,128)S(1)} %collective-permute-done.3), channel_id=1, source_target_pairs={{0,2},{1,7},{2,0},{3,5},{4,6},{5,3},{6,4},{7,1},{8,10},{9,15},{10,... | collective-permute-start | bytes 1474568 | tf_op jit(solution)/shard_map/ppermute | solution.py:51
  32.1 40.6 %collective-permute-start.11 = (f32[232,1280]{1,0:T(8,128)S(1)}, f32[232,1280]{1,0:T(8,128)S(1)}, u32[]{:S(2)}, u32[]{:S(2)}) collective-permute-start(f32[232,1280]{1,0:T(8,128)S(1)} %pad_maximum_fusion.4), channel_id=1, source_target_pairs={{0,16},{1,17},{2,18},{3,19},{4,20},{5,21},{6,22},{7,23},{8,24},{9,... | collective-permute-start | bytes 3563528 | tf_op jit(solution)/shard_map/ppermute | solution.py:51
  35.3 25.4 %copy-start.1 = (f32[2,224,1280]{2,1,0:T(8,128)}, f32[2,224,1280]{2,1,0:T(8,128)S(1)}, u32[]{:S(2)}) copy-start(f32[2,224,1280]{2,1,0:T(8,128)S(1)} %pad_maximum_fusion.1.refs_1_.refs_2_.refs_3_) | copy-start | bytes 6881284
  35.4 18.7 %collective-permute-start.5 = (f32[128,1280]{1,0:T(8,128)S(1)}, f32[128,1280]{1,0:T(8,128)S(1)}, u32[]{:S(2)}, u32[]{:S(2)}) collective-permute-start(f32[128,1280]{1,0:T(8,128)S(1)} %collective-permute-done.2), channel_id=1, source_target_pairs={{0,0},{1,97},{2,2},{3,99},{4,36},{5,69},{6,38},{7,71},{8,72},{9,41... | collective-permute-start | bytes 1966088 | tf_op jit(solution)/shard_map/ppermute | solution.py:51
  40.8 47.3 %collective-permute-start.14 = (f32[2,224,1280]{2,1,0:T(8,128)S(1)}, f32[2,224,1280]{2,1,0:T(8,128)S(1)}, u32[]{:S(2)}, u32[]{:S(2)}) collective-permute-start(f32[2,224,1280]{2,1,0:T(8,128)S(1)} %pad_maximum_fusion.1.refs_1_.refs_2_.refs_3_), channel_id=1, source_target_pairs={{0,96},{1,33},{2,98},{3,35},{4,100},{5,37},{6,102},{7,39},{8,104},... | collective-permute-start | bytes 6881288 | tf_op jit(solution)/shard_map/ppermute | solution.py:51
  46.1 15.6 %collective-permute-start.10 = (f32[96,1280]{1,0:T(8,128)S(1)}, f32[96,1280]{1,0:T(8,128)S(1)}, u32[]{:S(2)}, u32[]{:S(2)}) collective-permute-start(f32[96,1280]{1,0:T(8,128)S(1)} %collective-permute-done.6), channel_id=1, source_target_pairs={{0,2},{1,7},{2,0},{3,5},{4,6},{5,3},{6,4},{7,1},{8,10},{9,15},{10,... | collective-permute-start | bytes 1474568 | tf_op jit(solution)/shard_map/ppermute | solution.py:51
  47.6 27.3 %collective-permute-start.12 = (f32[2,96,1280]{2,1,0:T(8,128)S(1)}, f32[2,96,1280]{2,1,0:T(8,128)S(1)}, u32[]{:S(2)}, u32[]{:S(2)}) collective-permute-start(f32[2,96,1280]{2,1,0:T(8,128)S(1)} %pad_maximum_fusion.5), channel_id=1, source_target_pairs={{0,6},{1,3},{2,4},{3,1},{4,2},{5,7},{6,0},{7,5},{8,14},{9,11},{10,... | collective-permute-start | bytes 2949128 | tf_op jit(solution)/shard_map/ppermute | solution.py:51
  54.0 20.7 %collective-permute-start.9 = (f32[128,1280]{1,0:T(8,128)S(1)}, f32[128,1280]{1,0:T(8,128)S(1)}, u32[]{:S(2)}, u32[]{:S(2)}) collective-permute-start(f32[128,1280]{1,0:T(8,128)S(1)} %collective-permute-done.5), channel_id=1, source_target_pairs={{0,2},{1,7},{2,0},{3,5},{4,6},{5,3},{6,4},{7,1},{8,10},{9,15},{10,... | collective-permute-start | bytes 1966088 | tf_op jit(solution)/shard_map/ppermute | solution.py:51
  61.7 27.5 %collective-permute-start.8 = (f32[128,1280]{1,0:T(8,128)S(1)}, f32[128,1280]{1,0:T(8,128)S(1)}, u32[]{:S(2)}, u32[]{:S(2)}) collective-permute-start(f32[128,1280]{1,0:T(8,128)S(1)} %collective-permute-done.5), channel_id=1, source_target_pairs={{0,8},{1,9},{2,10},{3,11},{4,12},{5,13},{6,14},{7,15},{8,0},{9,1},... | collective-permute-start | bytes 1966088 | tf_op jit(solution)/shard_map/ppermute | solution.py:51
  72.8 20.1 %copy-start.2 = (f32[232,1280]{1,0:T(8,128)}, f32[232,1280]{1,0:T(8,128)S(1)}, u32[]{:S(2)}) copy-start(f32[232,1280]{1,0:T(8,128)S(1)} %fusion.2) | copy-start | bytes 3563524
  72.9 16.7 %collective-permute-start.15 = (f32[232,1280]{1,0:T(8,128)S(1)}, f32[232,1280]{1,0:T(8,128)S(1)}, u32[]{:S(2)}, u32[]{:S(2)}) collective-permute-start(f32[232,1280]{1,0:T(8,128)S(1)} %fusion.2), channel_id=1, source_target_pairs={{0,32},{1,97},{2,34},{3,99},{4,36},{5,101},{6,38},{7,103},{8,40},{... | collective-permute-start | bytes 3563528 | tf_op jit(solution)/shard_map/ppermute | solution.py:51
  74.8 13.3 %collective-permute-start.13 = (f32[2,96,1280]{2,1,0:T(8,128)S(1)}, f32[2,96,1280]{2,1,0:T(8,128)S(1)}, u32[]{:S(2)}, u32[]{:S(2)}) collective-permute-start(f32[2,96,1280]{2,1,0:T(8,128)S(1)} %pad_maximum_fusion.6), channel_id=1, source_target_pairs={{0,6},{1,3},{2,4},{3,1},{4,2},{5,7},{6,0},{7,5},{8,14},{9,11},{10,... | collective-permute-start | bytes 2949128 | tf_op jit(solution)/shard_map/ppermute | solution.py:51
  88.2 6.5 %copy-start.7 = (f32[2,224,1280]{2,1,0:T(8,128)}, f32[2,224,1280]{2,1,0:T(8,128)S(1)}, u32[]{:S(2)}) copy-start(f32[2,224,1280]{2,1,0:T(8,128)S(1)} %collective-permute-done.14.refs_3_.refs_4_.refs_5_) | copy-start | bytes 6881284
  88.2 22.9 %collective-permute-start.17 = (f32[2,128,1280]{2,1,0:T(8,128)S(1)}, f32[2,128,1280]{2,1,0:T(8,128)S(1)}, u32[]{:S(2)}, u32[]{:S(2)}) collective-permute-start(f32[2,128,1280]{2,1,0:T(8,128)S(1)} %pad_maximum_fusion.2), channel_id=1, source_target_pairs={{0,6},{1,3},{2,4},{3,1},{4,2},{5,7},{6,0},{7,5},{8,14},{9,11},{10,... | collective-permute-start | bytes 3932168 | tf_op jit(solution)/shard_map/ppermute | solution.py:51
  89.7 21.6 %copy-start.3 = (f32[232,1280]{1,0:T(8,128)}, f32[232,1280]{1,0:T(8,128)S(1)}, u32[]{:S(2)}) copy-start(f32[232,1280]{1,0:T(8,128)S(1)} %collective-permute-done.15) | copy-start | bytes 3563524
  89.7 15.8 %collective-permute-start.16 = (f32[128,1280]{1,0:T(8,128)S(1)}, f32[128,1280]{1,0:T(8,128)S(1)}, u32[]{:S(2)}, u32[]{:S(2)}) collective-permute-start(f32[128,1280]{1,0:T(8,128)S(1)} %collective-permute-done.8), channel_id=1, source_target_pairs={{0,2},{1,7},{2,0},{3,5},{4,6},{5,3},{6,4},{7,1},{8,10},{9,15},{10,... | collective-permute-start | bytes 1966088 | tf_op jit(solution)/shard_map/ppermute | solution.py:51
  92.9 2.7 %copy-start = (f32[2,4,96,1280]{3,2,1,0:T(8,128)}, f32[2,4,96,1280]{3,2,1,0:T(8,128)S(1)}, u32[]{:S(2)}) copy-start(f32[2,4,96,1280]{3,2,1,0:T(8,128)S(1)} %bitcast_dynamic-update-slice_fusion.6.refs_0_) | copy-start | bytes 11796484
  95.7 36.2 %collective-permute-start.19 = (f32[2,232,1280]{2,1,0:T(8,128)}, f32[2,232,1280]{2,1,0:T(8,128)}, u32[]{:S(2)}, u32[]{:S(2)}) collective-permute-start(f32[2,232,1280]{2,1,0:T(8,128)} %pad_maximum_fusion.refs_6_.refs_7_), channel_id=1, source_target_pairs={{0,96},{1,33},{2,98},{3,35},{4,100},{5,37},{6,102},{7,39},{8,104},... | collective-permute-start | bytes 7127048 | tf_op jit(solution)/shard_map/ppermute | solution.py:51
  111.0 16.9 %collective-permute-start.18 = (f32[2,128,1280]{2,1,0:T(8,128)S(1)}, f32[2,128,1280]{2,1,0:T(8,128)}, u32[]{:S(2)}, u32[]{:S(2)}) collective-permute-start(f32[2,128,1280]{2,1,0:T(8,128)S(1)} %pad_maximum_fusion.3), channel_id=1, source_target_pairs={{0,6},{1,3},{2,4},{3,1},{4,2},{5,7},{6,0},{7,5},{8,14},{9,11},{10,... | collective-permute-start | bytes 3932168 | tf_op jit(solution)/shard_map/ppermute | solution.py:51
  156.6 13.4 %collective-permute-start.20 = (f32[1280,640]{1,0:T(8,128)}, f32[1280,640]{1,0:T(8,128)S(1)}, u32[]{:S(2)}, u32[]{:S(2)}) collective-permute-start(f32[1280,640]{1,0:T(8,128)} %get-tuple-element.141), channel_id=1, source_target_pairs={{0,1},{1,0},{2,3},{3,2},{4,5},{5,4},{6,7},{7,6},{8,9},{9,8},{10,11... | collective-permute-start | bytes 9830408 | tf_op jit(solution)/shard_map/ppermute | solution.py:51
  165.0 3.7 %collective-permute-start.21 = (f32[640]{0:T(1024)S(1)}, f32[640]{0:T(1024)S(1)}, u32[]{:S(2)}, u32[]{:S(2)}) collective-permute-start(f32[640]{0:T(1024)S(1)} %dynamic_slice.23), channel_id=1, source_target_pairs={{0,1},{1,0},{2,3},{3,2},{4,5},{5,4},{6,7},{7,6},{8,9},{9,8},{10,11... | collective-permute-start | bytes 7688 | tf_op jit(solution)/shard_map/ppermute | solution.py:51

commit v3 on v2

--- a/solution.py
+++ b/solution.py
@@ -24,13 +24,13 @@
     ('X2', 'X1'),
     ('FOa', 'NOa'),
     ('NPa', 'ZHa'),
+    ('NOb', 'T2b'),
     ('ZHb', 'T2b'),
-    ('NOb', 'T2b'),
+    ('FPa', 'NPa', 'FOa'),
     ('V1', 'Z'),
-    ('FPa', 'NPa', 'FOa'),
-    ('FOb', 'NOb', 'FPa', 'X2'),
-    ('NPb', 'ZHb', 'V1'),
-    ('V2', 'V1'),
+    ('FOb', 'NOb'),
+    ('NPb', 'ZHb', 'FPa'),
+    ('V2', 'V1', 'X2'),
     ('FPb', 'NPb', 'FOb'),
 )
 
@@ -95,7 +95,10 @@
 def contract(left, right):
     left_high, left_low = in_two(left.reshape(-1, left.shape[-1]))
     right_high, right_low = in_two(right.reshape(-1, right.shape[-1]))
-    return dot(left_high, right_high) + (dot(left_low, right_high) + dot(left_high, right_low))
+    return dot(
+        jnp.concatenate([left_high, left_low, left_high], 0),
+        jnp.concatenate([right_high, right_high, right_low], 0),
+    )
 
 
 def accumulate(low, steps, based, pick_ref, *refs):

time: 177 us -> 177 us (level); the launches traced: 174 us -> 177 us
  starting transfers between devices: 43.5 us -> 47.4 us
  Pallas kernels: 35.2 us -> 33 us
    ppermute x22, starting transfers between devices: 43.5 us -> 47.4 us  [send(): return lax.ppermute(value, NAMES, pairs)]
    pallas_call x2, Pallas kernels: 35.2 us -> 33 us  [product(): pl.pallas_call(functools.partial(accumulate, low, steps, len(base) > 0),...]
  transfers between devices with their start and end apart: 22 -> 22, of which waited for: 13 -> 14; matrix products, arithmetic and copies ran while one was open for 12% -> 12% of each run, Pallas kernels for 6% -> 5%
where the time goes in v3:
time: 177 us
  waiting for transfers between devices  68.6 us (39%)
  starting transfers between devices  47.4 us (27%)
  Pallas kernels  33 us (19%)
  local copies, waits for them, and re-layouts  15.7 us (9%)
  other arithmetic  11 us (6%)
    ppermute x22, waiting for transfers between devices, send(): return lax.ppermute(value, NAMES, pairs)  68.6 us
    ppermute x22, starting transfers between devices, send(): return lax.ppermute(value, NAMES, pairs)  47.4 us
    pallas_call x2, Pallas kernels, product(): pl.pallas_call(functools.partial(accumulate, low, steps, len(base) > 0),...  33 us
    dynamic_update_slice x16, local copies, waits for them, and re-layouts, place(): lax.dynamic_update_slice(out, block[None, None, :shape[2]], (one, two, 0,...  9.58 us
    add x2, other arithmetic, body(): return (ours + send(theirs, flip_core), gradient + token[0, 0])  5.28 us
  transfers between devices with their start and end apart: 22, of which 14 were waited for; matrix products, arithmetic and copies ran while one was open for 12% of the time, Pallas kernels for 5%

profile of v3, /device:TPU:39, one launch (start us, length us, event | category | flops | bytes accessed | tf_op | source)
XLA Modules:
  0.0 176.7 jit_solution(5719260510405186842)
XLA Ops:
  0.7 1.3 constant_dynamic-slice_fusion
  4.9 2.7 %collective-permute-start.1 = (f32[96,1280]{1,0:T(8,128)S(1)}, f32[96,1280]{1,0:T(8,128)S(1)}, u32[]{:S(2)}, u32[]{:S(2)}) collective-permute-start(f32[96,1280]{1,0:T(8,128)S(1)} %slice_multiply_fusion.1), channel_id=1, source_target_pairs={{0,0},{1,13},{2,18},{3,31},{4,4},{5,9},{6,22},{7,27},{8,8},{9,5},{... | collective-permute-start | bytes 1474568 | tf_op jit(solution)/shard_map/ppermute | solution.py:51
  7.9 6.9 %collective-permute-done.1 = f32[96,1280]{1,0:T(8,128)S(1)} collective-permute-done((f32[96,1280]{1,0:T(8,128)S(1)}, f32[96,1280]{1,0:T(8,128)S(1)}, u32[]{:S(2)}, u32[]{:S(2)}) %collective-permute-start.1) | collective-permute-done | bytes 491552 | tf_op jit(solution)/shard_map/ppermute | solution.py:51
  14.8 7.8 %collective-permute-start.3 = (f32[96,1280]{1,0:T(8,128)S(1)}, f32[96,1280]{1,0:T(8,128)S(1)}, u32[]{:S(2)}, u32[]{:S(2)}) collective-permute-start(f32[96,1280]{1,0:T(8,128)S(1)} %collective-permute-done.1), channel_id=1, source_target_pairs={{0,0},{1,97},{2,2},{3,99},{4,36},{5,69},{6,38},{7,71},{8,72},{9,41... | collective-permute-start | bytes 1474568 | tf_op jit(solution)/shard_map/ppermute | solution.py:51
  22.7 2.6 %collective-permute-start.2 = (f32[128,1280]{1,0:T(8,128)S(1)}, f32[128,1280]{1,0:T(8,128)S(1)}, u32[]{:S(2)}, u32[]{:S(2)}) collective-permute-start(f32[128,1280]{1,0:T(8,128)S(1)} %slice_multiply_fusion), channel_id=1, source_target_pairs={{0,0},{1,13},{2,18},{3,31},{4,4},{5,9},{6,22},{7,27},{8,8},{9,5},{... | collective-permute-start | bytes 1966088 | tf_op jit(solution)/shard_map/ppermute | solution.py:51
  25.3 3.4 %collective-permute-done.3 = f32[96,1280]{1,0:T(8,128)S(1)} collective-permute-done((f32[96,1280]{1,0:T(8,128)S(1)}, f32[96,1280]{1,0:T(8,128)S(1)}, u32[]{:S(2)}, u32[]{:S(2)}) %collective-permute-start.3) | collective-permute-done | bytes 491552 | tf_op jit(solution)/shard_map/ppermute | solution.py:51
  28.8 2.0 %collective-permute-start.6 = (f32[96,1280]{1,0:T(8,128)S(1)}, f32[96,1280]{1,0:T(8,128)S(1)}, u32[]{:S(2)}, u32[]{:S(2)}) collective-permute-start(f32[96,1280]{1,0:T(8,128)S(1)} %collective-permute-done.3), channel_id=1, source_target_pairs={{0,8},{1,9},{2,10},{3,11},{4,12},{5,13},{6,14},{7,15},{8,0},{9,1},... | collective-permute-start | bytes 1474568 | tf_op jit(solution)/shard_map/ppermute | solution.py:51
  32.1 2.9 %collective-permute-start.10 = (f32[232,1280]{1,0:T(8,128)S(1)}, f32[232,1280]{1,0:T(8,128)S(1)}, u32[]{:S(2)}, u32[]{:S(2)}) collective-permute-start(f32[232,1280]{1,0:T(8,128)S(1)} %pad_maximum_fusion.4), channel_id=1, source_target_pairs={{0,16},{1,17},{2,18},{3,19},{4,20},{5,21},{6,22},{7,23},{8,24},{9,... | collective-permute-start | bytes 3563528 | tf_op jit(solution)/shard_map/ppermute | solution.py:51
  35.4 5.5 %collective-permute-start.5 = (f32[128,1280]{1,0:T(8,128)S(1)}, f32[128,1280]{1,0:T(8,128)S(1)}, u32[]{:S(2)}, u32[]{:S(2)}) collective-permute-start(f32[128,1280]{1,0:T(8,128)S(1)} %collective-permute-done.2), channel_id=1, source_target_pairs={{0,0},{1,97},{2,2},{3,99},{4,36},{5,69},{6,38},{7,71},{8,72},{9,41... | collective-permute-start | bytes 1966088 | tf_op jit(solution)/shard_map/ppermute | solution.py:51
  40.9 2.2 %collective-permute-done.7 = f32[96,1280]{1,0:T(8,128)S(1)} collective-permute-done((f32[96,1280]{1,0:T(8,128)S(1)}, f32[96,1280]{1,0:T(8,128)S(1)}, u32[]{:S(2)}, u32[]{:S(2)}) %collective-permute-start.7) | collective-permute-done | bytes 491552 | tf_op jit(solution)/shard_map/ppermute | solution.py:51
  43.2 2.9 %collective-permute-done.6 = f32[96,1280]{1,0:T(8,128)S(1)} collective-permute-done((f32[96,1280]{1,0:T(8,128)S(1)}, f32[96,1280]{1,0:T(8,128)S(1)}, u32[]{:S(2)}, u32[]{:S(2)}) %collective-permute-start.6) | collective-permute-done | bytes 491552 | tf_op jit(solution)/shard_map/ppermute | solution.py:51
  46.1 1.5 collective-permute-start.11
  47.9 6.1 %collective-permute-done.5 = f32[128,1280]{1,0:T(8,128)S(1)} collective-permute-done((f32[128,1280]{1,0:T(8,128)S(1)}, f32[128,1280]{1,0:T(8,128)S(1)}, u32[]{:S(2)}, u32[]{:S(2)}) %collective-permute-start.5) | collective-permute-done | bytes 655392 | tf_op jit(solution)/shard_map/ppermute | solution.py:51
  54.0 2.8 %collective-permute-start.8 = (f32[128,1280]{1,0:T(8,128)S(1)}, f32[128,1280]{1,0:T(8,128)S(1)}, u32[]{:S(2)}, u32[]{:S(2)}) collective-permute-start(f32[128,1280]{1,0:T(8,128)S(1)} %collective-permute-done.5), channel_id=1, source_target_pairs={{0,8},{1,9},{2,10},{3,11},{4,12},{5,13},{6,14},{7,15},{8,0},{9,1},... | collective-permute-start | bytes 1966088 | tf_op jit(solution)/shard_map/ppermute | solution.py:51
  56.8 2.8 %broadcast_in_dim.91 = f32[2,4,128,1280]{3,2,1,0:T(8,128)} broadcast(f32[]{:T(128)} %constant.76.clone.1), dimensions={} | broadcast | bytes 5242884 | tf_op jit(solution)/shard_map/broadcast_in_dim | solution.py:163
  61.8 11.0 %collective-permute-done.10 = f32[232,1280]{1,0:T(8,128)S(1)} collective-permute-done((f32[232,1280]{1,0:T(8,128)S(1)}, f32[232,1280]{1,0:T(8,128)S(1)}, u32[]{:S(2)}, u32[]{:S(2)}) %collective-permute-start.10) | collective-permute-done | bytes 1187872 | tf_op jit(solution)/shard_map/ppermute | solution.py:51
  72.8 1.9 %collective-permute-done.9 = f32[128,1280]{1,0:T(8,128)S(1)} collective-permute-done((f32[128,1280]{1,0:T(8,128)S(1)}, f32[128,1280]{1,0:T(8,128)S(1)}, u32[]{:S(2)}, u32[]{:S(2)}) %collective-permute-start.9) | collective-permute-done | bytes 655392 | tf_op jit(solution)/shard_map/ppermute | solution.py:51
  74.9 1.6 collective-permute-start.15
  76.5 1.4 collective-permute-start.17
  79.0 6.5 %collective-permute-done.8 = f32[128,1280]{1,0:T(8,128)S(1)} collective-permute-done((f32[128,1280]{1,0:T(8,128)S(1)}, f32[128,1280]{1,0:T(8,128)S(1)}, u32[]{:S(2)}, u32[]{:S(2)}) %collective-permute-start.8) | collective-permute-done | bytes 655392 | tf_op jit(solution)/shard_map/ppermute | solution.py:51
  85.6 4.6 %collective-permute-done.13 = f32[2,96,1280]{2,1,0:T(8,128)S(1)} collective-permute-done((f32[2,96,1280]{2,1,0:T(8,128)S(1)}, f32[2,96,1280]{2,1,0:T(8,128)S(1)}, u32[]{:S(2)}, u32[]{:S(2)}) %collective-permute-start.13) | collective-permute-done | bytes 983072 | tf_op jit(solution)/shard_map/ppermute | solution.py:51
  91.7 2.9 %pad_maximum_fusion.refs_6_.refs_7_ = f32[2,232,1280]{2,1,0:T(8,128)} fusion(f32[1,232,1280]{2,1,0:T(8,128)} %bitcast.15, f32[1,232,1280]{2,1,0:T(8,128)S(1)} %bitcast_dynamic-update-slice_fusion.14), kind=kLoop, calls=%fused_computation | loop fusion | flops 593920 | bytes 4751360 | tf_op jit(solution)/shard_map/stack | solution.py:211
  94.7 13.5 %collective-permute-done.14 = f32[128,1280]{1,0:T(8,128)S(1)} collective-permute-done((f32[128,1280]{1,0:T(8,128)S(1)}, f32[128,1280]{1,0:T(8,128)S(1)}, u32[]{:S(2)}, u32[]{:S(2)}) %collective-permute-start.14) | collective-permute-done | bytes 655392 | tf_op jit(solution)/shard_map/ppermute | solution.py:51
  110.7 9.2 %shard_map.59 = (f32[1280,640]{1,0:T(8,128)}, f32[1280,640]{1,0:T(8,128)}) custom-call(s32[2]{0:T(128)} %pad_add_fusion.pick_ref, f32[2,4,96,1280]{3,2,1,0:T(8,128)} %copy-done, f32[2,224,1280]{2,1,0:T(8,128)} %copy-done.1, f32[2,224,1280]{2,1,0:T(8,128)} %copy-done.1, f32[2,224,1280]{2,1,0:T(8,128)} %copy-done.6, f32[2,224,1280]{2,1,0:T(8,128)} %copy-done.6), custom_call_target="tpu_custom_call" | custom-call | flops 3774873600 | bytes 3932160 | tf_op jit(solution)/shard_map/pallas_call | solution.py:142
  121.6 4.5 %collective-permute-done.18 = f32[2,128,1280]{2,1,0:T(8,128)} collective-permute-done((f32[2,128,1280]{2,1,0:T(8,128)S(1)}, f32[2,128,1280]{2,1,0:T(8,128)}, u32[]{:S(2)}, u32[]{:S(2)}) %collective-permute-start.18) | collective-permute-done | bytes 1310752 | tf_op jit(solution)/shard_map/ppermute | solution.py:51
  126.1 2.0 %fusion.1 = f32[2,4,128,1280]{3,2,1,0:T(8,128)} fusion(f32[2,4,128,1280]{3,2,1,0:T(8,128)} %bitcast_dynamic-update-slice_fusion, s32[]{:T(128)S(6)} %select_n.143, s32[]{:T(128)S(6)} %select_n.154, f32[2,128,1280]{2,1,0:T(8,128)} %collective-permute-done.18), kind=kLoop, calls=%fused_computation.13 | loop fusion | bytes 1310728 | tf_op jit(solution)/shard_map/dynamic_update_slice | solution.py:166
  128.1 2.0 %fusion.refs_1_ = f32[2,4,128,1280]{3,2,1,0:T(8,128)} fusion(f32[2,4,128,1280]{3,2,1,0:T(8,128)} %fusion.1, s32[]{:T(128)S(6)} %select_n.146, s32[]{:T(128)S(6)} %select_n.156, f32[2,128,1280]{2,1,0:T(8,128)} %collective-permute-done.18), kind=kLoop, calls=%fused_computation.11 | loop fusion | bytes 1310728 | tf_op jit(solution)/shard_map/dynamic_update_slice | solution.py:166
  130.0 23.8 %shard_map.60 = (f32[1280,640]{1,0:T(8,128)}, f32[1280,640]{1,0:T(8,128)}) custom-call(s32[2]{0:T(128)} %pad_add_fusion.pick_ref, f32[2,4,96,1280]{3,2,1,0:T(8,128)} %copy-done, f32[2,4,128,1280]{3,2,1,0:T(8,128)} %fusion.refs_1_, f32[2,224,1280]{2,1,0:T(8,128)} %copy-done.1, f32[2,224,1280]{2,1,0:T(8,128)} %copy-done.1, f32[2,224,1280]{2,1,0:T(8,128)} %copy-done.6, ...), custom_call_target="tpu_custom_call" | custom-call | flops 17616076800 | bytes 18350080 | tf_op jit(solution)/shard_map/pallas_call | solution.py:142
  153.9 12.0 %collective-permute-start.20 = (f32[1280,640]{1,0:T(8,128)}, f32[1280,640]{1,0:T(8,128)S(1)}, u32[]{:S(2)}, u32[]{:S(2)}) collective-permute-start(f32[1280,640]{1,0:T(8,128)} %get-tuple-element.139), channel_id=1, source_target_pairs={{0,1},{1,0},{2,3},{3,2},{4,5},{5,4},{6,7},{7,6},{8,9},{9,8},{10,11... | collective-permute-start | bytes 9830408 | tf_op jit(solution)/shard_map/ppermute | solution.py:51
  168.2 3.2 %collective-permute-done.21 = f32[640]{0:T(1024)S(1)} collective-permute-done((f32[640]{0:T(1024)S(1)}, f32[640]{0:T(1024)S(1)}, u32[]{:S(2)}, u32[]{:S(2)}) %collective-permute-start.21) | collective-permute-done | bytes 2592 | tf_op jit(solution)/shard_map/ppermute | solution.py:51
  171.4 1.3 add_add_fusion.1
  172.7 4.0 %add.204 = f32[1280,640]{1,0:T(8,128)} add(f32[1280,640]{1,0:T(8,128)} %get-tuple-element.138, f32[1280,640]{1,0:T(8,128)S(1)} %collective-permute-done.20) | non-fusion elementwise | flops 819200 | bytes 9830400 | tf_op jit(solution)/shard_map/add | solution.py:264
  (76 shorter events, 17.1 us)
Async XLA Ops:
  0.6 2.1 %copy-start.4 = (f32[3]{0:T(128)S(1)}, f32[3]{0:T(128)}, u32[]{:S(2)}) copy-start(f32[3]{0:T(128)} %param.10) | copy-start | bytes 40
  0.6 2.1 %copy-start.3 = (s32[448]{0:T(512)S(1)}, s32[448]{0:T(512)}, u32[]{:S(2)}) copy-start(s32[448]{0:T(512)} %param.9) | copy-start | bytes 5380
  0.7 2.2 %copy-start.5 = (f32[448]{0:T(512)S(1)}, f32[448]{0:T(512)}, u32[]{:S(2)}) copy-start(f32[448]{0:T(512)} %param.11) | copy-start | bytes 5380
  2.0 2.4 %collective-permute-start = (f32[224,640]{1,0:T(8,128)S(1)}, f32[224,640]{1,0:T(8,128)S(1)}, u32[]{:S(2)}, u32[]{:S(2)}) collective-permute-start(f32[224,640]{1,0:T(8,128)S(1)} %get-tuple-element.148), channel_id=1, source_target_pairs={{0,1},{1,0},{2,3},{3,2},{4,5},{5,4},{6,7},{7,6},{8,9},{9,8},{10,11... | collective-permute-start | bytes 1720328 | tf_op jit(solution)/shard_map/ppermute | solution.py:51
  4.5 27.6 %collective-permute-start.4 = (f32[224,1280]{1,0:T(8,128)S(1)}, f32[224,1280]{1,0:T(8,128)S(1)}, u32[]{:S(2)}, u32[]{:S(2)}) collective-permute-start(f32[224,1280]{1,0:T(8,128)S(1)} %get-tuple-element.145), channel_id=1, source_target_pairs={{0,32},{1,97},{2,34},{3,99},{4,36},{5,101},{6,38},{7,103},{8,40},{... | collective-permute-start | bytes 3440648 | tf_op jit(solution)/shard_map/ppermute | solution.py:51
  4.9 9.9 %collective-permute-start.1 = (f32[96,1280]{1,0:T(8,128)S(1)}, f32[96,1280]{1,0:T(8,128)S(1)}, u32[]{:S(2)}, u32[]{:S(2)}) collective-permute-start(f32[96,1280]{1,0:T(8,128)S(1)} %slice_multiply_fusion.1), channel_id=1, source_target_pairs={{0,0},{1,13},{2,18},{3,31},{4,4},{5,9},{6,22},{7,27},{8,8},{9,5},{... | collective-permute-start | bytes 1474568 | tf_op jit(solution)/shard_map/ppermute | solution.py:51
  14.8 14.0 %collective-permute-start.3 = (f32[96,1280]{1,0:T(8,128)S(1)}, f32[96,1280]{1,0:T(8,128)S(1)}, u32[]{:S(2)}, u32[]{:S(2)}) collective-permute-start(f32[96,1280]{1,0:T(8,128)S(1)} %collective-permute-done.1), channel_id=1, source_target_pairs={{0,0},{1,97},{2,2},{3,99},{4,36},{5,69},{6,38},{7,71},{8,72},{9,41... | collective-permute-start | bytes 1474568 | tf_op jit(solution)/shard_map/ppermute | solution.py:51
  22.7 12.7 %collective-permute-start.2 = (f32[128,1280]{1,0:T(8,128)S(1)}, f32[128,1280]{1,0:T(8,128)S(1)}, u32[]{:S(2)}, u32[]{:S(2)}) collective-permute-start(f32[128,1280]{1,0:T(8,128)S(1)} %slice_multiply_fusion), channel_id=1, source_target_pairs={{0,0},{1,13},{2,18},{3,31},{4,4},{5,9},{6,22},{7,27},{8,8},{9,5},{... | collective-permute-start | bytes 1966088 | tf_op jit(solution)/shard_map/ppermute | solution.py:51
  28.8 17.3 %collective-permute-start.6 = (f32[96,1280]{1,0:T(8,128)S(1)}, f32[96,1280]{1,0:T(8,128)S(1)}, u32[]{:S(2)}, u32[]{:S(2)}) collective-permute-start(f32[96,1280]{1,0:T(8,128)S(1)} %collective-permute-done.3), channel_id=1, source_target_pairs={{0,8},{1,9},{2,10},{3,11},{4,12},{5,13},{6,14},{7,15},{8,0},{9,1},... | collective-permute-start | bytes 1474568 | tf_op jit(solution)/shard_map/ppermute | solution.py:51
  30.8 12.3 %collective-permute-start.7 = (f32[96,1280]{1,0:T(8,128)S(1)}, f32[96,1280]{1,0:T(8,128)S(1)}, u32[]{:S(2)}, u32[]{:S(2)}) collective-permute-start(f32[96,1280]{1,0:T(8,128)S(1)} %collective-permute-done.3), channel_id=1, source_target_pairs={{0,2},{1,7},{2,0},{3,5},{4,6},{5,3},{6,4},{7,1},{8,10},{9,15},{10,... | collective-permute-start | bytes 1474568 | tf_op jit(solution)/shard_map/ppermute | solution.py:51
  32.1 40.6 %collective-permute-start.10 = (f32[232,1280]{1,0:T(8,128)S(1)}, f32[232,1280]{1,0:T(8,128)S(1)}, u32[]{:S(2)}, u32[]{:S(2)}) collective-permute-start(f32[232,1280]{1,0:T(8,128)S(1)} %pad_maximum_fusion.4), channel_id=1, source_target_pairs={{0,16},{1,17},{2,18},{3,19},{4,20},{5,21},{6,22},{7,23},{8,24},{9,... | collective-permute-start | bytes 3563528 | tf_op jit(solution)/shard_map/ppermute | solution.py:51
  35.3 24.2 %copy-start.1 = (f32[2,224,1280]{2,1,0:T(8,128)}, f32[2,224,1280]{2,1,0:T(8,128)S(1)}, u32[]{:S(2)}) copy-start(f32[2,224,1280]{2,1,0:T(8,128)S(1)} %pad_maximum_fusion.1.refs_1_.refs_2_.refs_3_) | copy-start | bytes 6881284
  35.4 18.7 %collective-permute-start.5 = (f32[128,1280]{1,0:T(8,128)S(1)}, f32[128,1280]{1,0:T(8,128)S(1)}, u32[]{:S(2)}, u32[]{:S(2)}) collective-permute-start(f32[128,1280]{1,0:T(8,128)S(1)} %collective-permute-done.2), channel_id=1, source_target_pairs={{0,0},{1,97},{2,2},{3,99},{4,36},{5,69},{6,38},{7,71},{8,72},{9,41... | collective-permute-start | bytes 1966088 | tf_op jit(solution)/shard_map/ppermute | solution.py:51
  40.8 53.8 %collective-permute-start.16 = (f32[2,224,1280]{2,1,0:T(8,128)S(1)}, f32[2,224,1280]{2,1,0:T(8,128)S(1)}, u32[]{:S(2)}, u32[]{:S(2)}) collective-permute-start(f32[2,224,1280]{2,1,0:T(8,128)S(1)} %pad_maximum_fusion.1.refs_1_.refs_2_.refs_3_), channel_id=1, source_target_pairs={{0,96},{1,33},{2,98},{3,35},{4,100},{5,37},{6,102},{7,39},{8,104},... | collective-permute-start | bytes 6881288 | tf_op jit(solution)/shard_map/ppermute | solution.py:51
  46.1 14.3 %collective-permute-start.11 = (f32[96,1280]{1,0:T(8,128)S(1)}, f32[96,1280]{1,0:T(8,128)S(1)}, u32[]{:S(2)}, u32[]{:S(2)}) collective-permute-start(f32[96,1280]{1,0:T(8,128)S(1)} %collective-permute-done.6), channel_id=1, source_target_pairs={{0,2},{1,7},{2,0},{3,5},{4,6},{5,3},{6,4},{7,1},{8,10},{9,15},{10,... | collective-permute-start | bytes 1474568 | tf_op jit(solution)/shard_map/ppermute | solution.py:51
  47.6 27.3 %collective-permute-start.12 = (f32[2,96,1280]{2,1,0:T(8,128)S(1)}, f32[2,96,1280]{2,1,0:T(8,128)S(1)}, u32[]{:S(2)}, u32[]{:S(2)}) collective-permute-start(f32[2,96,1280]{2,1,0:T(8,128)S(1)} %pad_maximum_fusion.5), channel_id=1, source_target_pairs={{0,6},{1,3},{2,4},{3,1},{4,2},{5,7},{6,0},{7,5},{8,14},{9,11},{10,... | collective-permute-start | bytes 2949128 | tf_op jit(solution)/shard_map/ppermute | solution.py:51
  54.0 31.6 %collective-permute-start.8 = (f32[128,1280]{1,0:T(8,128)S(1)}, f32[128,1280]{1,0:T(8,128)S(1)}, u32[]{:S(2)}, u32[]{:S(2)}) collective-permute-start(f32[128,1280]{1,0:T(8,128)S(1)} %collective-permute-done.5), channel_id=1, source_target_pairs={{0,8},{1,9},{2,10},{3,11},{4,12},{5,13},{6,14},{7,15},{8,0},{9,1},... | collective-permute-start | bytes 1966088 | tf_op jit(solution)/shard_map/ppermute | solution.py:51
  60.4 14.3 %collective-permute-start.9 = (f32[128,1280]{1,0:T(8,128)S(1)}, f32[128,1280]{1,0:T(8,128)S(1)}, u32[]{:S(2)}, u32[]{:S(2)}) collective-permute-start(f32[128,1280]{1,0:T(8,128)S(1)} %collective-permute-done.5), channel_id=1, source_target_pairs={{0,2},{1,7},{2,0},{3,5},{4,6},{5,3},{6,4},{7,1},{8,10},{9,15},{10,... | collective-permute-start | bytes 1966088 | tf_op jit(solution)/shard_map/ppermute | solution.py:51
  72.8 17.6 %copy-start.2 = (f32[232,1280]{1,0:T(8,128)}, f32[232,1280]{1,0:T(8,128)S(1)}, u32[]{:S(2)}) copy-start(f32[232,1280]{1,0:T(8,128)S(1)} %fusion.2) | copy-start | bytes 3563524
  74.8 15.3 %collective-permute-start.13 = (f32[2,96,1280]{2,1,0:T(8,128)S(1)}, f32[2,96,1280]{2,1,0:T(8,128)S(1)}, u32[]{:S(2)}, u32[]{:S(2)}) collective-permute-start(f32[2,96,1280]{2,1,0:T(8,128)S(1)} %pad_maximum_fusion.6), channel_id=1, source_target_pairs={{0,6},{1,3},{2,4},{3,1},{4,2},{5,7},{6,0},{7,5},{8,14},{9,11},{10,... | collective-permute-start | bytes 2949128 | tf_op jit(solution)/shard_map/ppermute | solution.py:51
  74.9 16.7 %collective-permute-start.15 = (f32[232,1280]{1,0:T(8,128)S(1)}, f32[232,1280]{1,0:T(8,128)}, u32[]{:S(2)}, u32[]{:S(2)}) collective-permute-start(f32[232,1280]{1,0:T(8,128)S(1)} %fusion.2), channel_id=1, source_target_pairs={{0,32},{1,97},{2,34},{3,99},{4,36},{5,101},{6,38},{7,103},{8,40},{... | collective-permute-start | bytes 3563528 | tf_op jit(solution)/shard_map/ppermute | solution.py:51
  76.5 31.8 %collective-permute-start.17 = (f32[2,128,1280]{2,1,0:T(8,128)S(1)}, f32[2,128,1280]{2,1,0:T(8,128)S(1)}, u32[]{:S(2)}, u32[]{:S(2)}) collective-permute-start(f32[2,128,1280]{2,1,0:T(8,128)S(1)} %pad_maximum_fusion.2), channel_id=1, source_target_pairs={{0,6},{1,3},{2,4},{3,1},{4,2},{5,7},{6,0},{7,5},{8,14},{9,11},{10,... | collective-permute-start | bytes 3932168 | tf_op jit(solution)/shard_map/ppermute | solution.py:51
  90.1 18.0 %collective-permute-start.14 = (f32[128,1280]{1,0:T(8,128)S(1)}, f32[128,1280]{1,0:T(8,128)S(1)}, u32[]{:S(2)}, u32[]{:S(2)}) collective-permute-start(f32[128,1280]{1,0:T(8,128)S(1)} %collective-permute-done.8), channel_id=1, source_target_pairs={{0,2},{1,7},{2,0},{3,5},{4,6},{5,3},{6,4},{7,1},{8,10},{9,15},{10,... | collective-permute-start | bytes 1966088 | tf_op jit(solution)/shard_map/ppermute | solution.py:51
  90.4 4.2 %copy-start = (f32[2,4,96,1280]{3,2,1,0:T(8,128)}, f32[2,4,96,1280]{3,2,1,0:T(8,128)S(1)}, u32[]{:S(2)}) copy-start(f32[2,4,96,1280]{3,2,1,0:T(8,128)S(1)} %bitcast_dynamic-update-slice_fusion.6.refs_0_) | copy-start | bytes 11796484
  94.6 14.3 %copy-start.6 = (f32[2,224,1280]{2,1,0:T(8,128)}, f32[2,224,1280]{2,1,0:T(8,128)S(1)}, u32[]{:S(2)}) copy-start(f32[2,224,1280]{2,1,0:T(8,128)S(1)} %collective-permute-done.16.refs_3_.refs_4_.refs_5_) | copy-start | bytes 6881284
  94.6 35.4 %collective-permute-start.19 = (f32[2,232,1280]{2,1,0:T(8,128)}, f32[2,232,1280]{2,1,0:T(8,128)}, u32[]{:S(2)}, u32[]{:S(2)}) collective-permute-start(f32[2,232,1280]{2,1,0:T(8,128)} %pad_maximum_fusion.refs_6_.refs_7_), channel_id=1, source_target_pairs={{0,96},{1,33},{2,98},{3,35},{4,100},{5,37},{6,102},{7,39},{8,104},... | collective-permute-start | bytes 7127048 | tf_op jit(solution)/shard_map/ppermute | solution.py:51
  108.3 17.8 %collective-permute-start.18 = (f32[2,128,1280]{2,1,0:T(8,128)S(1)}, f32[2,128,1280]{2,1,0:T(8,128)}, u32[]{:S(2)}, u32[]{:S(2)}) collective-permute-start(f32[2,128,1280]{2,1,0:T(8,128)S(1)} %pad_maximum_fusion.3), channel_id=1, source_target_pairs={{0,6},{1,3},{2,4},{3,1},{4,2},{5,7},{6,0},{7,5},{8,14},{9,11},{10,... | collective-permute-start | bytes 3932168 | tf_op jit(solution)/shard_map/ppermute | solution.py:51
  153.9 18.8 %collective-permute-start.20 = (f32[1280,640]{1,0:T(8,128)}, f32[1280,640]{1,0:T(8,128)S(1)}, u32[]{:S(2)}, u32[]{:S(2)}) collective-permute-start(f32[1280,640]{1,0:T(8,128)} %get-tuple-element.139), channel_id=1, source_target_pairs={{0,1},{1,0},{2,3},{3,2},{4,5},{5,4},{6,7},{7,6},{8,9},{9,8},{10,11... | collective-permute-start | bytes 9830408 | tf_op jit(solution)/shard_map/ppermute | solution.py:51
  167.7 3.7 %collective-permute-start.21 = (f32[640]{0:T(1024)S(1)}, f32[640]{0:T(1024)S(1)}, u32[]{:S(2)}, u32[]{:S(2)}) collective-permute-start(f32[640]{0:T(1024)S(1)} %dynamic_slice.23), channel_id=1, source_target_pairs={{0,1},{1,0},{2,3},{3,2},{4,5},{5,4},{6,7},{7,6},{8,9},{9,8},{10,11... | collective-permute-start | bytes 7688 | tf_op jit(solution)/shard_map/ppermute | solution.py:51

commit v4 on v3

--- a/solution.py
+++ b/solution.py
@@ -101,8 +101,8 @@
     )
 
 
-def accumulate(low, steps, based, pick_ref, *refs):
-    lefts, rights, outs = refs[: len(low)], refs[len(low) : len(low) + 2 * CORE * len(steps)], refs[-CORE:]
+def accumulate(low, steps, based, many_sides, pick_ref, *refs):
+    lefts, rights, outs = refs[: len(low)], refs[len(low) : len(low) + 2 * many_sides * len(steps)], refs[-many_sides:]
     step = pl.program_id(1)
     columns = outs[0].shape[-1]
 
@@ -112,13 +112,13 @@
         first, last = low[named[0]], low[named[-1]] + lefts[named[-1]].shape[2]
         pairs = []
         for pair in range(2):
-            at = 2 * CORE * i + CORE * pair
-            pairs.append(jnp.concatenate([rights[at + side][:, first:last] for side in range(CORE)], 2))
+            at = 2 * many_sides * i + many_sides * pair
+            pairs.append(jnp.concatenate([rights[at + side][:, first:last] for side in range(many_sides)], 2))
         term = contract(left, jnp.concatenate(pairs, 0))
         for side, out_ref in enumerate(outs):
             part = term[:, side * columns : (side + 1) * columns]
             if based and i == 0:
-                part = part + refs[len(low) + 2 * CORE * len(steps) + side][...]
+                part = part + refs[len(low) + 2 * many_sides * len(steps) + side][...]
             out_ref[...] = part if i == 0 else out_ref[...] + part
 
     for i in range(len(steps)):
@@ -127,6 +127,7 @@
 
 def product(lefts, low, rights, sides, steps, base=()):
     columns = rights[0].shape[-1] // CORE
+    many_sides = sides.shape[0]
     rows, many = sum(left.shape[2] for left in lefts), len(steps)
 
     def left_spec(k, left):
@@ -140,23 +141,23 @@
 
     half = pl.BlockSpec((columns, columns), lambda h, i, pick: (h, 0))
     return pl.pallas_call(
-        functools.partial(accumulate, low, steps, len(base) > 0),
+        functools.partial(accumulate, low, steps, len(base) > 0, many_sides),
         grid_spec=pltpu.PrefetchScalarGridSpec(
             num_scalar_prefetch=1,
             grid=(CORE, many),
             in_specs=[left_spec(k, left) for k, left in enumerate(lefts)]
-            + [right_spec(right, side) for right in rights for side in range(CORE)]
+            + [right_spec(right, side) for right in rights for side in range(many_sides)]
             + [half] * len(base),
-            out_specs=[half] * CORE,
+            out_specs=[half] * many_sides,
         ),
-        out_shape=[jax.ShapeDtypeStruct((CORE * columns, columns), jnp.float32)] * CORE,
+        out_shape=[jax.ShapeDtypeStruct((CORE * columns, columns), jnp.float32)] * many_sides,
         compiler_params=pltpu.CompilerParams(vmem_limit_bytes=61 * 2**20),
         cost_estimate=pl.CostEstimate(
             flops=48 * many * rows * CORE * columns * columns,
             bytes_accessed=64 * many * rows * columns,
             transcendentals=0,
         ),
-    )(sides, *lefts, *(right for right in rights for _ in range(CORE)), *base)
+    )(sides, *lefts, *(right for right in rights for _ in range(many_sides)), *base)
 
 
 def place(buffer, shape, blocks):
@@ -260,8 +261,10 @@
     base = product([first], rows[:1], [sent["X2"], got["X2"]], sides, [([0], 0)])
     rights = [sent["X2"], got["X2"], sent["V2"], got["V2"]]
     steps = [([1], 0), ([0, 1], 1)]
-    theirs, ours = product([first, late], rows, rights, sides, steps, base)
-    return ours + send(theirs, flip_core), gradient + token[0, 0]
+    (theirs,) = product([first, late], rows, rights, sides[:1], steps, base[:1])
+    swapped = send(theirs, flip_core)
+    (ours,) = product([first, late], rows, rights, sides[1:], steps, base[1:])
+    return ours + swapped, gradient + token[0, 0]
 
 
 def solution(mesh):

time: 177 us -> 185 us (1.045)
  Pallas kernels: 33 us -> 40.4 us
    pallas_call x2 -> x3, Pallas kernels: 33 us -> 40.4 us  [product(): pl.pallas_call(functools.partial(accumulate, low, steps, len(base) > 0, m...]
  transfers between devices with their start and end apart: 22 -> 22, of which waited for: 14 -> 13; matrix products, arithmetic and copies ran while one was open for 12% -> 11% of each run, Pallas kernels for 5% -> 14%
where the time goes in v4:
time: 185 us
  waiting for transfers between devices  68.1 us (37%)
  starting transfers between devices  48.5 us (26%)
  Pallas kernels  40.4 us (22%)
  local copies, waits for them, and re-layouts  16.4 us (9%)
  other arithmetic  10.3 us (6%)
    ppermute x22, waiting for transfers between devices, send(): return lax.ppermute(value, NAMES, pairs)  68.1 us
    ppermute x22, starting transfers between devices, send(): return lax.ppermute(value, NAMES, pairs)  48.5 us
    pallas_call x3, Pallas kernels, product(): pl.pallas_call(functools.partial(accumulate, low, steps, len(base) > 0, m...  40.4 us
    dynamic_update_slice x16, local copies, waits for them, and re-layouts, place(): lax.dynamic_update_slice(out, block[None, None, :shape[2]], (one, two, 0,...  9.59 us
    add x2, other arithmetic, body(): return (ours + swapped, gradient + token[0, 0])  6.26 us
  transfers between devices with their start and end apart: 22, of which 13 were waited for; matrix products, arithmetic and copies ran while one was open for 11% of the time, Pallas kernels for 14%

profile of v4, /device:TPU:39, one launch (start us, length us, event | category | flops | bytes accessed | tf_op | source)
XLA Modules:
  0.0 184.6 jit_solution(14112103218146910367)
XLA Ops:
  0.7 1.3 constant_dynamic-slice_fusion
  4.9 2.7 %collective-permute-start.1 = (f32[96,1280]{1,0:T(8,128)S(1)}, f32[96,1280]{1,0:T(8,128)S(1)}, u32[]{:S(2)}, u32[]{:S(2)}) collective-permute-start(f32[96,1280]{1,0:T(8,128)S(1)} %slice_multiply_fusion.1), channel_id=1, source_target_pairs={{0,0},{1,13},{2,18},{3,31},{4,4},{5,9},{6,22},{7,27},{8,8},{9,5},{... | collective-permute-start | bytes 1474568 | tf_op jit(solution)/shard_map/ppermute | solution.py:51
  7.9 6.9 %collective-permute-done.1 = f32[96,1280]{1,0:T(8,128)S(1)} collective-permute-done((f32[96,1280]{1,0:T(8,128)S(1)}, f32[96,1280]{1,0:T(8,128)S(1)}, u32[]{:S(2)}, u32[]{:S(2)}) %collective-permute-start.1) | collective-permute-done | bytes 491552 | tf_op jit(solution)/shard_map/ppermute | solution.py:51
  14.8 7.8 %collective-permute-start.3 = (f32[96,1280]{1,0:T(8,128)S(1)}, f32[96,1280]{1,0:T(8,128)S(1)}, u32[]{:S(2)}, u32[]{:S(2)}) collective-permute-start(f32[96,1280]{1,0:T(8,128)S(1)} %collective-permute-done.1), channel_id=1, source_target_pairs={{0,0},{1,97},{2,2},{3,99},{4,36},{5,69},{6,38},{7,71},{8,72},{9,41... | collective-permute-start | bytes 1474568 | tf_op jit(solution)/shard_map/ppermute | solution.py:51
  22.7 2.6 %collective-permute-start.2 = (f32[128,1280]{1,0:T(8,128)S(1)}, f32[128,1280]{1,0:T(8,128)S(1)}, u32[]{:S(2)}, u32[]{:S(2)}) collective-permute-start(f32[128,1280]{1,0:T(8,128)S(1)} %slice_multiply_fusion), channel_id=1, source_target_pairs={{0,0},{1,13},{2,18},{3,31},{4,4},{5,9},{6,22},{7,27},{8,8},{9,5},{... | collective-permute-start | bytes 1966088 | tf_op jit(solution)/shard_map/ppermute | solution.py:51
  25.3 3.4 %collective-permute-done.3 = f32[96,1280]{1,0:T(8,128)S(1)} collective-permute-done((f32[96,1280]{1,0:T(8,128)S(1)}, f32[96,1280]{1,0:T(8,128)S(1)}, u32[]{:S(2)}, u32[]{:S(2)}) %collective-permute-start.3) | collective-permute-done | bytes 491552 | tf_op jit(solution)/shard_map/ppermute | solution.py:51
  28.8 2.0 %collective-permute-start.6 = (f32[96,1280]{1,0:T(8,128)S(1)}, f32[96,1280]{1,0:T(8,128)S(1)}, u32[]{:S(2)}, u32[]{:S(2)}) collective-permute-start(f32[96,1280]{1,0:T(8,128)S(1)} %collective-permute-done.3), channel_id=1, source_target_pairs={{0,8},{1,9},{2,10},{3,11},{4,12},{5,13},{6,14},{7,15},{8,0},{9,1},... | collective-permute-start | bytes 1474568 | tf_op jit(solution)/shard_map/ppermute | solution.py:51
  32.1 2.9 %collective-permute-start.10 = (f32[232,1280]{1,0:T(8,128)S(1)}, f32[232,1280]{1,0:T(8,128)S(1)}, u32[]{:S(2)}, u32[]{:S(2)}) collective-permute-start(f32[232,1280]{1,0:T(8,128)S(1)} %pad_maximum_fusion.4), channel_id=1, source_target_pairs={{0,16},{1,17},{2,18},{3,19},{4,20},{5,21},{6,22},{7,23},{8,24},{9,... | collective-permute-start | bytes 3563528 | tf_op jit(solution)/shard_map/ppermute | solution.py:51
  35.4 5.5 %collective-permute-start.5 = (f32[128,1280]{1,0:T(8,128)S(1)}, f32[128,1280]{1,0:T(8,128)S(1)}, u32[]{:S(2)}, u32[]{:S(2)}) collective-permute-start(f32[128,1280]{1,0:T(8,128)S(1)} %collective-permute-done.2), channel_id=1, source_target_pairs={{0,0},{1,97},{2,2},{3,99},{4,36},{5,69},{6,38},{7,71},{8,72},{9,41... | collective-permute-start | bytes 1966088 | tf_op jit(solution)/shard_map/ppermute | solution.py:51
  40.9 2.2 %collective-permute-done.7 = f32[96,1280]{1,0:T(8,128)S(1)} collective-permute-done((f32[96,1280]{1,0:T(8,128)S(1)}, f32[96,1280]{1,0:T(8,128)S(1)}, u32[]{:S(2)}, u32[]{:S(2)}) %collective-permute-start.7) | collective-permute-done | bytes 491552 | tf_op jit(solution)/shard_map/ppermute | solution.py:51
  43.2 2.9 %collective-permute-done.6 = f32[96,1280]{1,0:T(8,128)S(1)} collective-permute-done((f32[96,1280]{1,0:T(8,128)S(1)}, f32[96,1280]{1,0:T(8,128)S(1)}, u32[]{:S(2)}, u32[]{:S(2)}) %collective-permute-start.6) | collective-permute-done | bytes 491552 | tf_op jit(solution)/shard_map/ppermute | solution.py:51
  46.1 1.5 collective-permute-start.11
  47.9 6.1 %collective-permute-done.5 = f32[128,1280]{1,0:T(8,128)S(1)} collective-permute-done((f32[128,1280]{1,0:T(8,128)S(1)}, f32[128,1280]{1,0:T(8,128)S(1)}, u32[]{:S(2)}, u32[]{:S(2)}) %collective-permute-start.5) | collective-permute-done | bytes 655392 | tf_op jit(solution)/shard_map/ppermute | solution.py:51
  54.0 2.8 %collective-permute-start.8 = (f32[128,1280]{1,0:T(8,128)S(1)}, f32[128,1280]{1,0:T(8,128)S(1)}, u32[]{:S(2)}, u32[]{:S(2)}) collective-permute-start(f32[128,1280]{1,0:T(8,128)S(1)} %collective-permute-done.5), channel_id=1, source_target_pairs={{0,8},{1,9},{2,10},{3,11},{4,12},{5,13},{6,14},{7,15},{8,0},{9,1},... | collective-permute-start | bytes 1966088 | tf_op jit(solution)/shard_map/ppermute | solution.py:51
  56.8 2.8 %broadcast_in_dim.91 = f32[2,4,128,1280]{3,2,1,0:T(8,128)} broadcast(f32[]{:T(128)} %constant.76.clone.1), dimensions={} | broadcast | bytes 5242884 | tf_op jit(solution)/shard_map/broadcast_in_dim | solution.py:164
  61.8 11.0 %collective-permute-done.10 = f32[232,1280]{1,0:T(8,128)S(1)} collective-permute-done((f32[232,1280]{1,0:T(8,128)S(1)}, f32[232,1280]{1,0:T(8,128)S(1)}, u32[]{:S(2)}, u32[]{:S(2)}) %collective-permute-start.10) | collective-permute-done | bytes 1187872 | tf_op jit(solution)/shard_map/ppermute | solution.py:51
  72.8 1.9 %collective-permute-done.9 = f32[128,1280]{1,0:T(8,128)S(1)} collective-permute-done((f32[128,1280]{1,0:T(8,128)S(1)}, f32[128,1280]{1,0:T(8,128)S(1)}, u32[]{:S(2)}, u32[]{:S(2)}) %collective-permute-start.9) | collective-permute-done | bytes 655392 | tf_op jit(solution)/shard_map/ppermute | solution.py:51
  75.0 1.6 collective-permute-start.15
  76.5 1.4 collective-permute-start.17
  79.1 6.5 %collective-permute-done.8 = f32[128,1280]{1,0:T(8,128)S(1)} collective-permute-done((f32[128,1280]{1,0:T(8,128)S(1)}, f32[128,1280]{1,0:T(8,128)S(1)}, u32[]{:S(2)}, u32[]{:S(2)}) %collective-permute-start.8) | collective-permute-done | bytes 655392 | tf_op jit(solution)/shard_map/ppermute | solution.py:51
  85.6 4.5 %collective-permute-done.13 = f32[2,96,1280]{2,1,0:T(8,128)S(1)} collective-permute-done((f32[2,96,1280]{2,1,0:T(8,128)S(1)}, f32[2,96,1280]{2,1,0:T(8,128)S(1)}, u32[]{:S(2)}, u32[]{:S(2)}) %collective-permute-start.13) | collective-permute-done | bytes 983072 | tf_op jit(solution)/shard_map/ppermute | solution.py:51
  90.3 1.4 collective-permute-done.15
  91.7 1.8 pad_maximum_fusion.refs_4_
  93.6 14.5 %collective-permute-done.14 = f32[128,1280]{1,0:T(8,128)S(1)} collective-permute-done((f32[128,1280]{1,0:T(8,128)S(1)}, f32[128,1280]{1,0:T(8,128)S(1)}, u32[]{:S(2)}, u32[]{:S(2)}) %collective-permute-start.14) | collective-permute-done | bytes 655392 | tf_op jit(solution)/shard_map/ppermute | solution.py:51
  110.9 9.2 %shard_map.59 = (f32[1280,640]{1,0:T(8,128)}, f32[1280,640]{1,0:T(8,128)}) custom-call(s32[2]{0:T(128)} %copy-done.5, f32[2,4,96,1280]{3,2,1,0:T(8,128)} %copy-done, f32[2,224,1280]{2,1,0:T(8,128)} %copy-done.1, f32[2,224,1280]{2,1,0:T(8,128)} %copy-done.1, f32[2,224,1280]{2,1,0:T(8,128)} %copy-done.8, f32[2,224,1280]{2,1,0:T(8,128)} %copy-done.8), custom_call_target="tpu_custom_call" | custom-call | flops 3774873600 | bytes 3932160 | tf_op jit(solution)/shard_map/pallas_call | solution.py:143
  121.9 5.6 %collective-permute-done.18 = f32[2,128,1280]{2,1,0:T(8,128)} collective-permute-done((f32[2,128,1280]{2,1,0:T(8,128)S(1)}, f32[2,128,1280]{2,1,0:T(8,128)}, u32[]{:S(2)}, u32[]{:S(2)}) %collective-permute-start.18) | collective-permute-done | bytes 1310752 | tf_op jit(solution)/shard_map/ppermute | solution.py:51
  127.4 2.0 %fusion.1 = f32[2,4,128,1280]{3,2,1,0:T(8,128)} fusion(f32[2,4,128,1280]{3,2,1,0:T(8,128)} %bitcast_dynamic-update-slice_fusion, s32[]{:T(128)S(6)} %select_n.143, s32[]{:T(128)S(6)} %select_n.154, f32[2,128,1280]{2,1,0:T(8,128)} %collective-permute-done.18), kind=kLoop, calls=%fused_computation.13 | loop fusion | bytes 1310728 | tf_op jit(solution)/shard_map/dynamic_update_slice | solution.py:167
  129.4 2.0 %fusion.refs_1_ = f32[2,4,128,1280]{3,2,1,0:T(8,128)} fusion(f32[2,4,128,1280]{3,2,1,0:T(8,128)} %fusion.1, s32[]{:T(128)S(6)} %select_n.146, s32[]{:T(128)S(6)} %select_n.156, f32[2,128,1280]{2,1,0:T(8,128)} %collective-permute-done.18), kind=kLoop, calls=%fused_computation.11 | loop fusion | bytes 1310728 | tf_op jit(solution)/shard_map/dynamic_update_slice | solution.py:167
  131.4 15.4 %shard_map.61 = f32[1280,640]{1,0:T(8,128)} custom-call(s32[1]{0:T(128)} %get-tuple-element.146.pick_ref, f32[2,4,96,1280]{3,2,1,0:T(8,128)} %copy-done, f32[2,4,128,1280]{3,2,1,0:T(8,128)} %fusion.refs_1_, f32[2,224,1280]{2,1,0:T(8,128)} %copy-done.1, f32[2,224,1280]{2,1,0:T(8,128)} %copy-done.8, f32[2,232,1280]{2,1,0:T(8,128)} %pad_maximum_fusion.refs_4_, ...), custom_call_target="tpu_custom_call" | custom-call | flops 17616076800 | bytes 18350080 | tf_op jit(solution)/shard_map/pallas_call | solution.py:143
  146.8 13.4 %collective-permute-start.20 = (f32[1280,640]{1,0:T(8,128)}, f32[1280,640]{1,0:T(8,128)}, u32[]{:S(2)}, u32[]{:S(2)}) collective-permute-start(f32[1280,640]{1,0:T(8,128)} %shard_map.61), channel_id=1, source_target_pairs={{0,1},{1,0},{2,3},{3,2},{4,5},{5,4},{6,7},{7,6},{8,9},{9,8},{10,11... | collective-permute-start | bytes 9830408 | tf_op jit(solution)/shard_map/ppermute | solution.py:51
  162.5 15.8 %shard_map.60 = f32[1280,640]{1,0:T(8,128)} custom-call(s32[1]{0:T(128)} %get-tuple-element.147.pick_ref, f32[2,4,96,1280]{3,2,1,0:T(8,128)} %copy-done, f32[2,4,128,1280]{3,2,1,0:T(8,128)} %fusion.refs_1_, f32[2,224,1280]{2,1,0:T(8,128)} %copy-done.1, f32[2,224,1280]{2,1,0:T(8,128)} %copy-done.8, f32[2,232,1280]{2,1,0:T(8,128)} %pad_maximum_fusion.refs_4_, ...), custom_call_target="tpu_custom_call" | custom-call | flops 17616076800 | bytes 18350080 | tf_op jit(solution)/shard_map/pallas_call | solution.py:143
  179.7 5.0 %add.204 = f32[1280,640]{1,0:T(8,128)} add(f32[1280,640]{1,0:T(8,128)} %shard_map.60, f32[1280,640]{1,0:T(8,128)} %collective-permute-done.20) | non-fusion elementwise | flops 819200 | bytes 9830400 | tf_op jit(solution)/shard_map/add | solution.py:267
  (82 shorter events, 17.6 us)
Async XLA Ops:
  0.6 2.1 %copy-start.6 = (f32[3]{0:T(128)S(1)}, f32[3]{0:T(128)}, u32[]{:S(2)}) copy-start(f32[3]{0:T(128)} %param.10) | copy-start | bytes 40
  0.6 2.1 %copy-start.4 = (s32[448]{0:T(512)S(1)}, s32[448]{0:T(512)}, u32[]{:S(2)}) copy-start(s32[448]{0:T(512)} %param.9) | copy-start | bytes 5380
  0.7 2.2 %copy-start.7 = (f32[448]{0:T(512)S(1)}, f32[448]{0:T(512)}, u32[]{:S(2)}) copy-start(f32[448]{0:T(512)} %param.11) | copy-start | bytes 5380
  2.0 2.4 %collective-permute-start = (f32[224,640]{1,0:T(8,128)S(1)}, f32[224,640]{1,0:T(8,128)S(1)}, u32[]{:S(2)}, u32[]{:S(2)}) collective-permute-start(f32[224,640]{1,0:T(8,128)S(1)} %get-tuple-element.144), channel_id=1, source_target_pairs={{0,1},{1,0},{2,3},{3,2},{4,5},{5,4},{6,7},{7,6},{8,9},{9,8},{10,11... | collective-permute-start | bytes 1720328 | tf_op jit(solution)/shard_map/ppermute | solution.py:51
  3.1 106.9 %copy-start.5 = (s32[2]{0:T(128)}, s32[2]{0:T(128)S(1)}, u32[]{:S(2)}) copy-start(s32[2]{0:T(128)S(1)} %pad_add_fusion.pick_ref) | copy-start | bytes 28
  4.5 27.6 %collective-permute-start.4 = (f32[224,1280]{1,0:T(8,128)S(1)}, f32[224,1280]{1,0:T(8,128)S(1)}, u32[]{:S(2)}, u32[]{:S(2)}) collective-permute-start(f32[224,1280]{1,0:T(8,128)S(1)} %get-tuple-element.141), channel_id=1, source_target_pairs={{0,32},{1,97},{2,34},{3,99},{4,36},{5,101},{6,38},{7,103},{8,40},{... | collective-permute-start | bytes 3440648 | tf_op jit(solution)/shard_map/ppermute | solution.py:51
  4.9 9.9 %collective-permute-start.1 = (f32[96,1280]{1,0:T(8,128)S(1)}, f32[96,1280]{1,0:T(8,128)S(1)}, u32[]{:S(2)}, u32[]{:S(2)}) collective-permute-start(f32[96,1280]{1,0:T(8,128)S(1)} %slice_multiply_fusion.1), channel_id=1, source_target_pairs={{0,0},{1,13},{2,18},{3,31},{4,4},{5,9},{6,22},{7,27},{8,8},{9,5},{... | collective-permute-start | bytes 1474568 | tf_op jit(solution)/shard_map/ppermute | solution.py:51
  14.8 14.0 %collective-permute-start.3 = (f32[96,1280]{1,0:T(8,128)S(1)}, f32[96,1280]{1,0:T(8,128)S(1)}, u32[]{:S(2)}, u32[]{:S(2)}) collective-permute-start(f32[96,1280]{1,0:T(8,128)S(1)} %collective-permute-done.1), channel_id=1, source_target_pairs={{0,0},{1,97},{2,2},{3,99},{4,36},{5,69},{6,38},{7,71},{8,72},{9,41... | collective-permute-start | bytes 1474568 | tf_op jit(solution)/shard_map/ppermute | solution.py:51
  22.7 12.7 %collective-permute-start.2 = (f32[128,1280]{1,0:T(8,128)S(1)}, f32[128,1280]{1,0:T(8,128)S(1)}, u32[]{:S(2)}, u32[]{:S(2)}) collective-permute-start(f32[128,1280]{1,0:T(8,128)S(1)} %slice_multiply_fusion), channel_id=1, source_target_pairs={{0,0},{1,13},{2,18},{3,31},{4,4},{5,9},{6,22},{7,27},{8,8},{9,5},{... | collective-permute-start | bytes 1966088 | tf_op jit(solution)/shard_map/ppermute | solution.py:51
  28.8 17.3 %collective-permute-start.6 = (f32[96,1280]{1,0:T(8,128)S(1)}, f32[96,1280]{1,0:T(8,128)S(1)}, u32[]{:S(2)}, u32[]{:S(2)}) collective-permute-start(f32[96,1280]{1,0:T(8,128)S(1)} %collective-permute-done.3), channel_id=1, source_target_pairs={{0,8},{1,9},{2,10},{3,11},{4,12},{5,13},{6,14},{7,15},{8,0},{9,1},... | collective-permute-start | bytes 1474568 | tf_op jit(solution)/shard_map/ppermute | solution.py:51
  30.8 12.3 %collective-permute-start.7 = (f32[96,1280]{1,0:T(8,128)S(1)}, f32[96,1280]{1,0:T(8,128)S(1)}, u32[]{:S(2)}, u32[]{:S(2)}) collective-permute-start(f32[96,1280]{1,0:T(8,128)S(1)} %collective-permute-done.3), channel_id=1, source_target_pairs={{0,2},{1,7},{2,0},{3,5},{4,6},{5,3},{6,4},{7,1},{8,10},{9,15},{10,... | collective-permute-start | bytes 1474568 | tf_op jit(solution)/shard_map/ppermute | solution.py:51
  32.1 40.6 %collective-permute-start.10 = (f32[232,1280]{1,0:T(8,128)S(1)}, f32[232,1280]{1,0:T(8,128)S(1)}, u32[]{:S(2)}, u32[]{:S(2)}) collective-permute-start(f32[232,1280]{1,0:T(8,128)S(1)} %pad_maximum_fusion.4), channel_id=1, source_target_pairs={{0,16},{1,17},{2,18},{3,19},{4,20},{5,21},{6,22},{7,23},{8,24},{9,... | collective-permute-start | bytes 3563528 | tf_op jit(solution)/shard_map/ppermute | solution.py:51
  35.3 24.2 %copy-start.1 = (f32[2,224,1280]{2,1,0:T(8,128)}, f32[2,224,1280]{2,1,0:T(8,128)S(1)}, u32[]{:S(2)}) copy-start(f32[2,224,1280]{2,1,0:T(8,128)S(1)} %pad_maximum_fusion.1.refs_1_.refs_2_) | copy-start | bytes 6881284
  35.4 18.7 %collective-permute-start.5 = (f32[128,1280]{1,0:T(8,128)S(1)}, f32[128,1280]{1,0:T(8,128)S(1)}, u32[]{:S(2)}, u32[]{:S(2)}) collective-permute-start(f32[128,1280]{1,0:T(8,128)S(1)} %collective-permute-done.2), channel_id=1, source_target_pairs={{0,0},{1,97},{2,2},{3,99},{4,36},{5,69},{6,38},{7,71},{8,72},{9,41... | collective-permute-start | bytes 1966088 | tf_op jit(solution)/shard_map/ppermute | solution.py:51
  40.8 52.7 %collective-permute-start.16 = (f32[2,224,1280]{2,1,0:T(8,128)S(1)}, f32[2,224,1280]{2,1,0:T(8,128)S(1)}, u32[]{:S(2)}, u32[]{:S(2)}) collective-permute-start(f32[2,224,1280]{2,1,0:T(8,128)S(1)} %pad_maximum_fusion.1.refs_1_.refs_2_), channel_id=1, source_target_pairs={{0,96},{1,33},{2,98},{3,35},{4,100},{5,37},{6,102},{7,39},{8,104},... | collective-permute-start | bytes 6881288 | tf_op jit(solution)/shard_map/ppermute | solution.py:51
  46.1 14.3 %collective-permute-start.11 = (f32[96,1280]{1,0:T(8,128)S(1)}, f32[96,1280]{1,0:T(8,128)S(1)}, u32[]{:S(2)}, u32[]{:S(2)}) collective-permute-start(f32[96,1280]{1,0:T(8,128)S(1)} %collective-permute-done.6), channel_id=1, source_target_pairs={{0,2},{1,7},{2,0},{3,5},{4,6},{5,3},{6,4},{7,1},{8,10},{9,15},{10,... | collective-permute-start | bytes 1474568 | tf_op jit(solution)/shard_map/ppermute | solution.py:51
  47.6 27.3 %collective-permute-start.12 = (f32[2,96,1280]{2,1,0:T(8,128)S(1)}, f32[2,96,1280]{2,1,0:T(8,128)S(1)}, u32[]{:S(2)}, u32[]{:S(2)}) collective-permute-start(f32[2,96,1280]{2,1,0:T(8,128)S(1)} %pad_maximum_fusion.5), channel_id=1, source_target_pairs={{0,6},{1,3},{2,4},{3,1},{4,2},{5,7},{6,0},{7,5},{8,14},{9,11},{10,... | collective-permute-start | bytes 2949128 | tf_op jit(solution)/shard_map/ppermute | solution.py:51
  54.0 31.6 %collective-permute-start.8 = (f32[128,1280]{1,0:T(8,128)S(1)}, f32[128,1280]{1,0:T(8,128)S(1)}, u32[]{:S(2)}, u32[]{:S(2)}) collective-permute-start(f32[128,1280]{1,0:T(8,128)S(1)} %collective-permute-done.5), channel_id=1, source_target_pairs={{0,8},{1,9},{2,10},{3,11},{4,12},{5,13},{6,14},{7,15},{8,0},{9,1},... | collective-permute-start | bytes 1966088 | tf_op jit(solution)/shard_map/ppermute | solution.py:51
  60.4 14.3 %collective-permute-start.9 = (f32[128,1280]{1,0:T(8,128)S(1)}, f32[128,1280]{1,0:T(8,128)S(1)}, u32[]{:S(2)}, u32[]{:S(2)}) collective-permute-start(f32[128,1280]{1,0:T(8,128)S(1)} %collective-permute-done.5), channel_id=1, source_target_pairs={{0,2},{1,7},{2,0},{3,5},{4,6},{5,3},{6,4},{7,1},{8,10},{9,15},{10,... | collective-permute-start | bytes 1966088 | tf_op jit(solution)/shard_map/ppermute | solution.py:51
  72.8 6.0 %copy-start.2 = (f32[232,1280]{1,0:T(8,128)}, f32[232,1280]{1,0:T(8,128)S(1)}, u32[]{:S(2)}) copy-start(f32[232,1280]{1,0:T(8,128)S(1)} %fusion.2) | copy-start | bytes 3563524
  74.9 15.2 %collective-permute-start.13 = (f32[2,96,1280]{2,1,0:T(8,128)S(1)}, f32[2,96,1280]{2,1,0:T(8,128)S(1)}, u32[]{:S(2)}, u32[]{:S(2)}) collective-permute-start(f32[2,96,1280]{2,1,0:T(8,128)S(1)} %pad_maximum_fusion.6), channel_id=1, source_target_pairs={{0,6},{1,3},{2,4},{3,1},{4,2},{5,7},{6,0},{7,5},{8,14},{9,11},{10,... | collective-permute-start | bytes 2949128 | tf_op jit(solution)/shard_map/ppermute | solution.py:51
  75.0 16.7 %collective-permute-start.15 = (f32[232,1280]{1,0:T(8,128)S(1)}, f32[232,1280]{1,0:T(8,128)S(1)}, u32[]{:S(2)}, u32[]{:S(2)}) collective-permute-start(f32[232,1280]{1,0:T(8,128)S(1)} %fusion.2), channel_id=1, source_target_pairs={{0,32},{1,97},{2,34},{3,99},{4,36},{5,101},{6,38},{7,103},{8,40},{... | collective-permute-start | bytes 3563528 | tf_op jit(solution)/shard_map/ppermute | solution.py:51
  76.5 31.6 %collective-permute-start.17 = (f32[2,128,1280]{2,1,0:T(8,128)S(1)}, f32[2,128,1280]{2,1,0:T(8,128)S(1)}, u32[]{:S(2)}, u32[]{:S(2)}) collective-permute-start(f32[2,128,1280]{2,1,0:T(8,128)S(1)} %pad_maximum_fusion.2), channel_id=1, source_target_pairs={{0,6},{1,3},{2,4},{3,1},{4,2},{5,7},{6,0},{7,5},{8,14},{9,11},{10,... | collective-permute-start | bytes 3932168 | tf_op jit(solution)/shard_map/ppermute | solution.py:51
  90.1 18.0 %collective-permute-start.14 = (f32[128,1280]{1,0:T(8,128)S(1)}, f32[128,1280]{1,0:T(8,128)S(1)}, u32[]{:S(2)}, u32[]{:S(2)}) collective-permute-start(f32[128,1280]{1,0:T(8,128)S(1)} %collective-permute-done.8), channel_id=1, source_target_pairs={{0,2},{1,7},{2,0},{3,5},{4,6},{5,3},{6,4},{7,1},{8,10},{9,15},{10,... | collective-permute-start | bytes 1966088 | tf_op jit(solution)/shard_map/ppermute | solution.py:51
  90.3 3.2 %copy-start = (f32[2,4,96,1280]{3,2,1,0:T(8,128)}, f32[2,4,96,1280]{3,2,1,0:T(8,128)S(1)}, u32[]{:S(2)}) copy-start(f32[2,4,96,1280]{3,2,1,0:T(8,128)S(1)} %bitcast_dynamic-update-slice_fusion.6.refs_0_) | copy-start | bytes 11796484
  91.7 18.3 %copy-start.3 = (f32[232,1280]{1,0:T(8,128)}, f32[232,1280]{1,0:T(8,128)S(1)}, u32[]{:S(2)}) copy-start(f32[232,1280]{1,0:T(8,128)S(1)} %collective-permute-done.15) | copy-start | bytes 3563524
  93.5 16.5 %copy-start.8 = (f32[2,224,1280]{2,1,0:T(8,128)}, f32[2,224,1280]{2,1,0:T(8,128)S(1)}, u32[]{:S(2)}) copy-start(f32[2,224,1280]{2,1,0:T(8,128)S(1)} %collective-permute-done.16.refs_3_.refs_4_) | copy-start | bytes 6881284
  93.5 37.9 %collective-permute-start.19 = (f32[2,232,1280]{2,1,0:T(8,128)}, f32[2,232,1280]{2,1,0:T(8,128)}, u32[]{:S(2)}, u32[]{:S(2)}) collective-permute-start(f32[2,232,1280]{2,1,0:T(8,128)} %pad_maximum_fusion.refs_4_), channel_id=1, source_target_pairs={{0,96},{1,33},{2,98},{3,35},{4,100},{5,37},{6,102},{7,39},{8,104},... | collective-permute-start | bytes 7127048 | tf_op jit(solution)/shard_map/ppermute | solution.py:51
  110.6 16.9 %collective-permute-start.18 = (f32[2,128,1280]{2,1,0:T(8,128)S(1)}, f32[2,128,1280]{2,1,0:T(8,128)}, u32[]{:S(2)}, u32[]{:S(2)}) collective-permute-start(f32[2,128,1280]{2,1,0:T(8,128)S(1)} %pad_maximum_fusion.3), channel_id=1, source_target_pairs={{0,6},{1,3},{2,4},{3,1},{4,2},{5,7},{6,0},{7,5},{8,14},{9,11},{10,... | collective-permute-start | bytes 3932168 | tf_op jit(solution)/shard_map/ppermute | solution.py:51
  146.8 32.8 %collective-permute-start.20 = (f32[1280,640]{1,0:T(8,128)}, f32[1280,640]{1,0:T(8,128)}, u32[]{:S(2)}, u32[]{:S(2)}) collective-permute-start(f32[1280,640]{1,0:T(8,128)} %shard_map.61), channel_id=1, source_target_pairs={{0,1},{1,0},{2,3},{3,2},{4,5},{5,4},{6,7},{7,6},{8,9},{9,8},{10,11... | collective-permute-start | bytes 9830408 | tf_op jit(solution)/shard_map/ppermute | solution.py:51
  162.5 15.9 %collective-permute-start.21 = (f32[640]{0:T(1024)S(1)}, f32[640]{0:T(1024)S(1)}, u32[]{:S(2)}, u32[]{:S(2)}) collective-permute-start(f32[640]{0:T(1024)S(1)} %dynamic_slice.23), channel_id=1, source_target_pairs={{0,1},{1,0},{2,3},{3,2},{4,5},{5,4},{6,7},{7,6},{8,9},{9,8},{10,11... | collective-permute-start | bytes 7688 | tf_op jit(solution)/shard_map/ppermute | solution.py:51
